TPU v7x, 128 devices: a whole 4x4x4 slice. The times are simulated.
128 devices in a mesh: expert: 8 (over y, z_hi), tp: 16 (over x, z_lo, core).
Axes of the slice: x: 4, y: 4, z: 4 (z_hi: 2, z_lo: 2; z = z_hi * 2 + z_lo), core: 2. Of those that a mesh axis runs over, the one named last changes fastest.
Arguments:
- tokens: bfloat16 [2048, 3072], P(('expert', 'tp')), may hold values from -6 to 6
- routes: int32 [2048, 2], P(('expert', 'tp')), may hold values from 0 to 7, as said below
- counts: int32 [8], replicated, may hold values from 1 to 1536, as said below
- gate_weight: bfloat16 [8, 3072, 8192], P('expert', None, 'tp'), may hold values from -0.109375 to 0.109375
- up_weight: bfloat16 [8, 3072, 8192], P('expert', None, 'tp'), may hold values from -0.109375 to 0.109375
Outputs:
- hessian: float32 [8, 8192, 8192], P('expert', 'tp')
Inputs may be any that keep to these rules, and one draw needn't show every extreme that they name: `routes`: each row names two different experts. Among the 16 rows of one device no expert is named by more than 12 rows, and the same expert is named by exactly 12 rows on every device. counts[e] is the number of rows of routes that name expert e.
All inputs are finite; a program needn't handle non-finite values.
Results may differ from a plain program's by a relative error of at most 0.004.
Values may be sent and summed in bfloat16 or wider, within the bound.
No kernel may reach another device: no remote copies, remote signals or barrier semaphores. Data moves between devices by JAX's collectives and lax.ppermute only.
A program may use at most 128 MiB of HBM per device.

v0:
```python
import functools

import jax
import jax.numpy as jnp
from jax import lax
from jax.experimental import pallas as pl
from jax.experimental.pallas import tpu as pltpu
from jax.sharding import Mesh
from jax.sharding import PartitionSpec as P

AXES = ("y", "h", "x", "l", "c")
ROUTE_LANES = 128
VMEM_BYTES = 56 * 1024 * 1024
SLOTS = 12
INTERPRET = False
ANY = pl.BlockSpec(memory_space=pl.ANY)
SMEM = pl.BlockSpec(memory_space=pltpu.SMEM)
VMEM = pl.BlockSpec(memory_space=pltpu.VMEM)


def ring_hop(a, axis):
    pairs = [(2 * i + c, 2 * ((i + (1, 3)[c]) % 4) + c) for i in range(4) for c in range(2)]
    return lax.ppermute(a, (axis, "c"), pairs)


def ring_back(a, axis):
    pairs = [(2 * i + c, 2 * ((i + (3, 1)[c]) % 4) + c) for i in range(4) for c in range(2)]
    return lax.ppermute(a, (axis, "c"), pairs)


def swap(a, axis):
    return lax.ppermute(a, axis, [(0, 1), (1, 0)])


def far_swap(a):
    return lax.ppermute(a, ("h", "l"), [(0, 3), (3, 0), (1, 2), (2, 1)])


def after(a, *others):
    return lax.optimization_barrier((a,) + others)[0]


def tie(a, token):
    return lax.optimization_barrier((a, token))


def cost(microseconds):
    return pl.CostEstimate(
        flops=int(microseconds * 1_150_000_000), bytes_accessed=1_000_000, transcendentals=0
    )


def select_kernel(n, width, expert_ref, base_ref, *rest):
    sources, (own_ref, twin_ref, held, sems) = rest[:n], rest[n:]
    copies, row = [], 0
    for i, source in enumerate(sources):
        rows = pl.ds(row, source.shape[0])
        copies.append(pltpu.make_async_copy(source, held.at[rows], sems.at[i]))
        copies[-1].start()
        row += source.shape[0]
    tokens, out_rows = held.shape[0], 2 * own_ref.shape[1]
    first = lax.broadcasted_iota(jnp.int32, (tokens, tokens), 0)
    second = lax.broadcasted_iota(jnp.int32, (tokens, tokens), 1)
    earlier = jnp.logical_and(first // 16 == second // 16, first < second)
    earlier = earlier.astype(jnp.float32).astype(jnp.bfloat16)
    lane = lax.broadcasted_iota(jnp.int32, (tokens, ROUTE_LANES), 1)
    places = lax.broadcasted_iota(jnp.int32, (out_rows, tokens), 0).astype(jnp.float32)
    ones = jnp.ones((16, ROUTE_LANES), jnp.bfloat16)
    for copy in copies:
        copy.wait()
    named = held[:, width:].astype(jnp.float32) == expert_ref[0].astype(jnp.float32)
    named = jnp.logical_and(named, lane < 2).astype(jnp.float32).astype(jnp.bfloat16)
    named = lax.dot_general(
        ones, named, (((1,), (1,)), ((), ())), preferred_element_type=jnp.float32
    )
    rank = jnp.dot(named.astype(jnp.bfloat16), earlier, preferred_element_type=jnp.float32)
    place = jnp.where(named[0:1, :] > 0.5, base_ref[0:1, :] + rank[0:1, :], -1.0)
    pick = (places == place).astype(jnp.float32).astype(jnp.bfloat16)
    half = width // 2
    for side, start in ((0, half), (1, 0)):
        got = jnp.dot(pick, held[:, start : start + half], preferred_element_type=jnp.float32)
        got = got.astype(jnp.bfloat16)
        own_ref[side] = got[: out_rows // 2]
        twin_ref[side] = got[out_rows // 2 :]


def select(expert, base, blocks, width):
    tokens = sum(b.shape[0] for b in blocks)
    half = jax.ShapeDtypeStruct((2, tokens // 32 * SLOTS, width // 2), jnp.bfloat16)
    return pl.pallas_call(
        functools.partial(select_kernel, len(blocks), width),
        out_shape=(half, half),
        in_specs=[SMEM, VMEM] + [ANY] * len(blocks),
        out_specs=(VMEM, VMEM),
        scratch_shapes=[
            pltpu.VMEM((tokens, blocks[0].shape[1]), jnp.bfloat16),
            pltpu.SemaphoreType.DMA((len(blocks),)),
        ],
        compiler_params=pltpu.CompilerParams(vmem_limit_bytes=VMEM_BYTES),
        cost_estimate=cost(3),
        interpret=INTERPRET,
    )(expert, base, *blocks)


def ffn_kernel(blocks, n_arrays, n_old, offsets_ref, *rest):
    arrays, (gate_hbm, up_hbm) = rest[:n_arrays], rest[n_arrays : n_arrays + 2]
    (
        out_ref,
        token_ref,
        rows,
        gate_held,
        up_held,
        result,
        sems,
        weight_sems,
        out_sems,
    ) = rest[n_arrays + 2 + n_old :]
    token_ref[...] = jnp.zeros_like(token_ref)
    piece_rows = rows.shape[0] // len(blocks)
    width, half = rows.shape[1] // 2, gate_held.shape[1] // 2
    copies = []
    for i, parts in enumerate(blocks):
        for array, start, count in parts:
            for side in range(2):
                target = rows.at[
                    pl.ds(i * piece_rows + start, count), pl.ds(side * width, width)
                ]
                copies.append(
                    pltpu.make_async_copy(
                        arrays[array].at[1 - side], target, sems.at[len(copies)]
                    )
                )
    weight_copies = []
    for q in range(2):
        cols = pl.ds(q * half, half)
        for j, (src, dst) in enumerate(((gate_hbm, gate_held), (up_hbm, up_held))):
            weight_copies.append(
                pltpu.make_async_copy(src.at[:, cols], dst.at[:, cols], weight_sems.at[2 * q + j])
            )
    for copy in weight_copies[:2] + copies + weight_copies[2:]:
        copy.start()
    for copy in copies:
        copy.wait()
    sent = []
    for q in range(2):
        weight_copies[2 * q].wait()
        weight_copies[2 * q + 1].wait()
        cols = slice(q * half, (q + 1) * half)
        gate = jnp.dot(rows[...], gate_held[:, cols], preferred_element_type=jnp.float32)
        up = jnp.dot(rows[...], up_held[:, cols], preferred_element_type=jnp.float32)
        result[q] = (gate / (1.0 + jnp.exp(-gate)) * up).astype(jnp.bfloat16)
        for i in range(len(blocks)):
            to = pl.ds(pl.multiple_of(offsets_ref[i], 16), piece_rows)
            sent.append(
                pltpu.make_async_copy(
                    result.at[q, pl.ds(i * piece_rows, piece_rows)],
                    out_ref.at[1 - q, to],
                    out_sems.at[q, i],
                )
            )
            sent[-1].start()
    for copy in sent:
        copy.wait()


def indexed(blocks):
    arrays, sources = [], []
    for parts in blocks:
        sources.append([])
        start = 0
        for array in parts:
            at = [i for i, known in enumerate(arrays) if known is array]
            if not at:
                arrays.append(array)
                at = [len(arrays) - 1]
            sources[-1].append((at[0], start, array.shape[1]))
            start += array.shape[1]
    return arrays, sources, start


def ffn(offsets, blocks, wg, wu, total_rows, token, old=()):
    arrays, sources, piece_rows = indexed(blocks)
    width, panel = wg.shape
    rows = len(blocks) * piece_rows
    out = jax.ShapeDtypeStruct((2, total_rows, panel // 2), jnp.bfloat16)
    first_old = 4 + len(arrays)
    return pl.pallas_call(
        functools.partial(ffn_kernel, sources, len(arrays), len(old) + 1),
        out_shape=(out, jax.ShapeDtypeStruct((8, 128), jnp.float32)),
        in_specs=[SMEM] + [ANY] * (len(arrays) + 3 + len(old)),
        out_specs=(ANY, VMEM),
        scratch_shapes=[
            pltpu.VMEM((rows, width), jnp.bfloat16),
            pltpu.VMEM(wg.shape, jnp.bfloat16),
            pltpu.VMEM(wu.shape, jnp.bfloat16),
            pltpu.VMEM((2, rows, panel // 2), jnp.bfloat16),
            pltpu.SemaphoreType.DMA((2 * sum(len(parts) for parts in sources),)),
            pltpu.SemaphoreType.DMA((4,)),
            pltpu.SemaphoreType.DMA((2, len(blocks))),
        ],
        input_output_aliases={first_old + i: i for i in range(len(old))},
        compiler_params=pltpu.CompilerParams(vmem_limit_bytes=VMEM_BYTES),
        cost_estimate=cost(1),
        interpret=INTERPRET,
    )(offsets, *arrays, wg, wu, token, *old)


def gram_kernel(sources, n_arrays, first, extra, ids_ref, scale_ref, *rest):
    own_ref, *arrays = rest[: 1 + n_arrays]
    out_ref, token_ref, *rest = rest[1 + n_arrays + extra :]
    if first:
        turned, own_held, held, result, own_sem, in_sems, out_sems = rest
    else:
        turned, held, result, own_sem, in_sems, out_sems = rest
    token_ref[...] = jnp.zeros_like(token_ref)
    half = held.shape[3]
    depth, count = held.shape[0], len(sources)

    def fetch(p):
        copies = []
        for k, (array, start, rows) in enumerate(sources[p]):
            target = held.at[p % depth, :, pl.ds(start, rows)]
            copies.append(pltpu.make_async_copy(arrays[array], target, in_sems.at[p % depth, k]))
            copies[-1].start()
        return copies

    own = pltpu.make_async_copy(own_ref, own_held if first else turned, own_sem)
    own.start()
    fetched = {0: fetch(0)}
    own.wait()
    if first:
        for side in range(2):
            turned[side * half : (side + 1) * half, :] = own_held[1 - side].T
    fetched.update({p: fetch(p) for p in range(1, min(depth, count))})
    sent = {}
    for p in range(count):
        for copy in fetched[p]:
            copy.wait()
        if p >= 2:
            sent[p - 2].wait()
        for side in range(2):
            total = jnp.dot(
                turned[...], held[p % depth, 1 - side], preferred_element_type=jnp.float32
            )
            result[p % 2, :, side * half : (side + 1) * half] = total * scale_ref[0]
        if p + depth < count:
            fetched[p + depth] = fetch(p + depth)
        cols = pl.ds(pl.multiple_of(ids_ref[p] * 2 * half, 2 * half), 2 * half)
        sent[p] = pltpu.make_async_copy(result.at[p % 2], out_ref.at[:, cols], out_sems.at[p % 2])
        sent[p].start()
    for p in range(max(0, count - 2), count):
        sent[p].wait()


def gram(ids, scale, own, pairs, features, token, old=None):
    arrays, sources, rows = indexed(pairs)
    half = arrays[0].shape[2]
    first = own.ndim == 3
    extra = 1 if old is None else 2
    turned = ((2 * half, rows), jnp.bfloat16)
    return pl.pallas_call(
        functools.partial(gram_kernel, sources, len(arrays), first, extra),
        out_shape=(
            jax.ShapeDtypeStruct((2 * half, features), jnp.float32),
            jax.ShapeDtypeStruct((8, 128), jnp.float32),
        )
        + ((jax.ShapeDtypeStruct(*turned),) if first else ()),
        in_specs=[SMEM] * 2 + [ANY] * (1 + len(arrays) + extra),
        out_specs=(ANY, VMEM) + ((VMEM,) if first else ()),
        scratch_shapes=[
            pltpu.VMEM((2, rows, half), jnp.bfloat16) if first else pltpu.VMEM(*turned),
            pltpu.VMEM((3, 2, rows, half), jnp.bfloat16),
            pltpu.VMEM((2, 2 * half, 2 * half), jnp.float32),
            pltpu.SemaphoreType.DMA(()),
            pltpu.SemaphoreType.DMA((3, 2)),
            pltpu.SemaphoreType.DMA((2,)),
        ],
        input_output_aliases={} if old is None else {4 + len(arrays): 0},
        compiler_params=pltpu.CompilerParams(vmem_limit_bytes=VMEM_BYTES),
        cost_estimate=cost(1),
        interpret=INTERPRET,
    )(ids, scale, own, *arrays, token, *([] if old is None else [old]))


class Spread:
    def __init__(self):
        self.found = {}

    def keep(self, arrays, at, dl, core):
        twins = [swap(array, "c") for array in arrays]
        at_twin = {"o": "o", "m": "p", "f": "f"}[at]
        self.found[at, dl, core] = arrays
        self.found[at_twin, dl, 1 - core] = twins
        return twins

    def open(self, pair, twin=None):
        beside, near = swap(pair, "l"), ring_hop(pair, "x")
        if twin is None:
            twin = swap(pair, "c")
        near_twin = ring_hop(twin, "x")
        self.found["o", 0, 0], self.found["o", 0, 1] = [pair], [twin]
        self.moved = (beside, near, near_twin)

    def first(self, token):
        beside, near, near_twin = self.moved
        beside, near, token = lax.optimization_barrier((beside, near, token))
        self.moved = (beside, near, near_twin)
        return token

    def second(self):
        beside, near, near_twin = self.moved
        near_beside = swap(near, "l")
        far = ring_hop(near, "x")
        (twin,) = self.keep([beside], "o", 1, 0)
        beside_near = ring_hop(twin, "x")
        self.keep([near], "m", 0, 0)
        self.keep([near_twin], "m", 0, 1)
        self.moved = (far, near_beside, beside_near)

    def third(self, token):
        far, near_beside, beside_near = self.moved
        far, token = tie(far, token)
        rows = far.shape[1] // 3
        over_l = swap(far[:, :rows], "l")
        near_beside, token = tie(near_beside, token)
        over_x = ring_hop(near_beside[:, rows:], "x")
        self.keep([near_beside], "m", 1, 0)
        beside_near, token = tie(beside_near, token)
        self.keep([beside_near], "m", 1, 1)
        self.keep([far], "f", 0, 0)
        self.moved = (over_l, over_x)
        return token

    def end(self, token):
        *moved, token = lax.optimization_barrier((*self.moved, token))
        self.keep(moved, "f", 1, 0)
        return token


def local(tokens, routes, counts, gate_weight, up_weight):
    x, l, c = lax.axis_index("x"), lax.axis_index("l"), lax.axis_index("c")
    expert = lax.axis_index("y") * 2 + lax.axis_index("h")
    gate_panel, up_panel = gate_weight[0], up_weight[0]
    width, panel = gate_panel.shape
    features = 16 * panel
    routed_total = jnp.sum(jnp.where(jnp.arange(8) == expert, counts, 0)).astype(jnp.float32)
    scale = (2.0 / routed_total).reshape(1)
    expert = expert.reshape(1).astype(jnp.int32)

    tagged = jnp.concatenate(
        [tokens, jnp.pad(routes.astype(tokens.dtype), ((0, 0), (0, ROUTE_LANES - 2)))], axis=1
    )
    pair = jnp.stack([tagged, far_swap(tagged)])
    near, back = ring_hop(pair, "y"), ring_back(pair, "y")
    far = lax.ppermute(pair, "y", [(i, (i + 2) % 4) for i in range(4)])
    parts = [(a, swap(a, "c")) for a in (pair, near, back, far)]

    block = 8 * SLOTS
    y_near, y_back = 1 + c, 2 - c
    base = []
    for y_mine, y_twin in ((0, 0), (y_near, y_back), (y_back, y_near), (3, 3)):
        for dc, y_of in ((0, y_mine), (1, y_twin)):
            base += [dc * block + (2 * y_of + dh) * SLOTS for dh in (0, 1)]
    base = jnp.stack([jnp.asarray(b, jnp.int32) for b in base])
    base = jnp.broadcast_to(jnp.repeat(base, 16).astype(jnp.float32), (8, 256))
    blocks = [a.reshape((-1, a.shape[-1])) for part in parts for a in part]
    pair, twin = select(expert, base, blocks, width)

    place_of = {"o": x, "m": x - (1 - 2 * c), "p": x + (1 - 2 * c), "f": x + 2}

    def chip(at, dl):
        return (place_of[at] % 4) * 2 + (l + dl) % 2

    def offsets(chips):
        rows = [
            (chip(at, dl) * 2 + (c + half) % 2) * block for at, dl in chips for half in (0, 1)
        ]
        return jnp.stack(rows).astype(jnp.int32)

    def blocks_of(spread, chips):
        return [spread.found[at, dl, core] for at, dl in chips for core in (0, 1)]

    total = 16 * block

    def hidden_of(chips, token, *old):
        return ffn(
            offsets(chips), blocks_of(rows, chips), gate_panel, up_panel, total, token, old
        )

    token = jnp.zeros((8, 128), jnp.float32)
    rows = Spread()
    rows.open(pair, twin)
    hidden, token = hidden_of([("o", 0)], token)
    token = rows.first(token)
    rows.second()
    hidden, token = hidden_of([("o", 1), ("m", 0), ("p", 0)], token, hidden)
    token = rows.third(token)
    hidden, token = hidden_of([("m", 1), ("p", 1), ("f", 0)], token, hidden)
    token = rows.end(token)
    hidden, token = hidden_of([("f", 1)], token, hidden)

    def part(chips, token, old=None):
        ids = [chip(at, dl) * 2 + (c + core) % 2 for at, dl in chips for core in (0, 1)]
        ids = jnp.stack(ids).astype(jnp.int32)
        return gram(ids, scale, own, blocks_of(panels, chips), features, token, old)

    panels = Spread()
    panels.open(hidden)
    token = panels.first(token)
    panels.second()
    own = hidden
    out, token, own = part([("o", 0), ("o", 1), ("m", 0), ("p", 0)], token)
    token = panels.third(token)
    out, token = part([("m", 1), ("p", 1), ("f", 0)], token, out)
    token = panels.end(token)
    out, token = part([("f", 1)], token, out)
    return out[None]


def solution(mesh):
    fine = Mesh(mesh.devices.reshape(4, 2, 4, 2, 2), AXES)
    rows = P(AXES, None)
    weight = P(("y", "h"), None, ("x", "l", "c"))
    return jax.shard_map(
        local,
        mesh=fine,
        in_specs=(rows, rows, P(), weight, weight),
        out_specs=P(("y", "h"), ("x", "l", "c"), None),
        check_vma=False,
    )
```

profile of v0, /device:TPU:1, one launch (start us, length us, event | category | flops | bytes accessed | tf_op | source)
XLA Modules:
  0.0 197.8 jit_solution(15545850451446365297)
XLA Ops:
  1.7 4.7 %collective-permute-start = (bf16[16,3200]{1,0:T(8,128)(2,1)S(1)}, bf16[16,3200]{1,0:T(8,128)(2,1)S(1)}, u32[]{:S(2)}, u32[]{:S(2)}) collective-permute-start(bf16[16,3200]{1,0:T(8,128)(2,1)S(1)} %get-tuple-element.86), channel_id=1, source_target_pairs={{0,18},{18,0},{2,16},{16,2},{1,19},{19,1},{3,17},{17,3},{4,22},{22... | collective-permute-start | bytes 307208 | tf_op jit(solution)/shard_map/ppermute | solution.py:36
  6.4 2.6 %collective-permute-done = bf16[16,3200]{1,0:T(8,128)(2,1)S(1)} collective-permute-done((bf16[16,3200]{1,0:T(8,128)(2,1)S(1)}, bf16[16,3200]{1,0:T(8,128)(2,1)S(1)}, u32[]{:S(2)}, u32[]{:S(2)}) %collective-permute-start) | collective-permute-done | bytes 102432 | tf_op jit(solution)/shard_map/ppermute | solution.py:36
  9.0 2.8 %collective-permute-start.2 = (bf16[2,16,3200]{2,1,0:T(8,128)(2,1)S(1)}, bf16[2,16,3200]{2,1,0:T(8,128)(2,1)S(1)}, u32[]{:S(2)}, u32[]{:S(2)}) collective-permute-start(bf16[2,16,3200]{2,1,0:T(8,128)(2,1)S(1)} %pad_maximum_fusion), channel_id=1, source_target_pairs={{0,32},{1,97},{32,64},{33,1},{64,96},{65,33},{96,0},{97,65},{2,34}... | collective-permute-start | bytes 614408 | tf_op jit(solution)/shard_map/ppermute | solution.py:23
  13.5 2.1 %collective-permute-start.1 = (bf16[2,16,3200]{2,1,0:T(8,128)(2,1)S(1)}, bf16[2,16,3200]{2,1,0:T(8,128)(2,1)S(1)}, u32[]{:S(2)}, u32[]{:S(2)}) collective-permute-start(bf16[2,16,3200]{2,1,0:T(8,128)(2,1)S(1)} %pad_maximum_fusion), channel_id=1, source_target_pairs={{0,1},{1,0},{2,3},{3,2},{4,5},{5,4},{6,7},{7,6},{8,9},{9,8},{10,11... | collective-permute-start | bytes 614408 | tf_op jit(solution)/shard_map/ppermute | solution.py:32
  15.5 3.1 %collective-permute-start.3 = (bf16[2,16,3200]{2,1,0:T(8,128)(2,1)S(1)}, bf16[2,16,3200]{2,1,0:T(8,128)(2,1)S(1)}, u32[]{:S(2)}, u32[]{:S(2)}) collective-permute-start(bf16[2,16,3200]{2,1,0:T(8,128)(2,1)S(1)} %collective-permute-done.2), channel_id=1, source_target_pairs={{0,1},{1,0},{2,3},{3,2},{4,5},{5,4},{6,7},{7,6},{8,9},{9,8},{10,11... | collective-permute-start | bytes 614408 | tf_op jit(solution)/shard_map/ppermute | solution.py:32
  25.6 4.0 %shard_map.55 = (bf16[2,96,1536]{2,1,0:T(8,128)(2,1)}, bf16[2,96,1536]{2,1,0:T(8,128)(2,1)}) custom-call(s32[1]{0:T(128)} %bitcast.13.expert_ref, f32[8,256]{1,0:T(8,128)} %broadcast_in_dim.18.base_ref, bf16[32,3200]{1,0:T(8,128)(2,1)} %bitcast.64, bf16[32,3200]{1,0:T(8,128)(2,1)} %bitcast.69, bf16[32,3200]{1,0:T(8,128)(2,1)} %bitcast.66, ...), custom_call_target="tpu_custom_call" | custom-call | flops 3449999872 | bytes 1000000 | tf_op jit(solution)/shard_map/pallas_call | solution.py:90
  29.7 2.5 %collective-permute-start.9 = (bf16[2,96,1536]{2,1,0:T(8,128)(2,1)}, bf16[2,96,1536]{2,1,0:T(8,128)(2,1)S(1)}, u32[]{:S(2)}, u32[]{:S(2)}) collective-permute-start(bf16[2,96,1536]{2,1,0:T(8,128)(2,1)} %get-tuple-element.45.rest_0_), channel_id=1, source_target_pairs={{0,4},{1,13},{4,8},{5,1},{8,12},{9,5},{12,0},{13,9},{2,6},{3,15},{... | collective-permute-start | bytes 1769480 | tf_op jit(solution)/shard_map/ppermute | solution.py:23
  34.0 6.3 %shard_map.56 = (bf16[2,1536,256]{2,1,0:T(8,128)(2,1)}, f32[8,128]{1,0:T(8,128)}) custom-call(s32[2]{0:T(128)} %pad_add_fusion.2.offsets_ref, bf16[2,96,1536]{2,1,0:T(8,128)(2,1)} %get-tuple-element.45.rest_0_, bf16[2,96,1536]{2,1,0:T(8,128)(2,1)} %get-tuple-element.46.rest_1_, bf16[3072,512]{1,0:T(8,128)(2,1)} %bitcast.56, bf16[3072,512]{1,0:T(8,128)(2,1)} %bitcast.60, ...), custom_call_target="tpu_custom_call" | custom-call | flops 1150000000 | bytes 1000000 | tf_op jit(solution)/shard_map/pallas_call | solution.py:187
  40.2 4.2 %collective-permute-done.8.rest_0_ = bf16[2,96,1536]{2,1,0:T(8,128)(2,1)S(1)} collective-permute-done((bf16[2,96,1536]{2,1,0:T(8,128)(2,1)}, bf16[2,96,1536]{2,1,0:T(8,128)(2,1)S(1)}, u32[]{:S(2)}, u32[]{:S(2)}) %collective-permute-start.8) | collective-permute-done | bytes 589856 | tf_op jit(solution)/shard_map/ppermute | solution.py:32
  51.9 9.6 %shard_map.57 = (bf16[2,1536,256]{2,1,0:T(8,128)(2,1)}, f32[8,128]{1,0:T(8,128)}) custom-call(s32[6]{0:T(128)} %stack.189.offsets_ref, bf16[2,96,1536]{2,1,0:T(8,128)(2,1)} %copy-done.8, bf16[2,96,1536]{2,1,0:T(8,128)(2,1)} %collective-permute-done.11.rest_1_, bf16[2,96,1536]{2,1,0:T(8,128)(2,1)} %copy-done.7, ...), custom_call_target="tpu_custom_call", output_to_operand_aliasing={{0}: (10, {})} | custom-call | flops 1150000000 | bytes 1000000 | tf_op jit(solution)/shard_map/pallas_call | solution.py:187
  61.5 2.4 %collective-permute-done.16.rest_0_ = bf16[2,96,1536]{2,1,0:T(8,128)(2,1)S(1)} collective-permute-done((bf16[2,96,1536]{2,1,0:T(8,128)(2,1)S(1)}, bf16[2,96,1536]{2,1,0:T(8,128)(2,1)S(1)}, u32[]{:S(2)}, u32[]{:S(2)}) %collective-permute-start.16) | collective-permute-done | bytes 589856 | tf_op jit(solution)/shard_map/ppermute | solution.py:32
  70.9 9.6 %shard_map.58 = (bf16[2,1536,256]{2,1,0:T(8,128)(2,1)}, f32[8,128]{1,0:T(8,128)}) custom-call(s32[6]{0:T(128)} %stack.196.offsets_ref, bf16[2,96,1536]{2,1,0:T(8,128)(2,1)} %copy-done.2, bf16[2,96,1536]{2,1,0:T(8,128)(2,1)} %copy-done.9, bf16[2,96,1536]{2,1,0:T(8,128)(2,1)} %copy-done.13, ...), custom_call_target="tpu_custom_call", output_to_operand_aliasing={{0}: (10, {})} | custom-call | flops 1150000000 | bytes 1000000 | tf_op jit(solution)/shard_map/pallas_call | solution.py:187
  83.5 6.5 %shard_map.59 = (bf16[2,1536,256]{2,1,0:T(8,128)(2,1)}, f32[8,128]{1,0:T(8,128)}) custom-call(s32[2]{0:T(128)} %pad_add_fusion.1.offsets_ref, bf16[2,32,1536]{2,1,0:T(8,128)(2,1)} %collective-permute-done.15.rest_0_, bf16[2,64,1536]{2,1,0:T(8,128)(2,1)} %collective-permute-done.17.rest_1_, ...), custom_call_target="tpu_custom_call", output_to_operand_aliasing={{0}: (8, {})} | custom-call | flops 1150000000 | bytes 1000000 | tf_op jit(solution)/shard_map/pallas_call | solution.py:187
  90.5 2.3 %collective-permute-start.26 = (bf16[2,1536,256]{2,1,0:T(8,128)(2,1)}, bf16[2,1536,256]{2,1,0:T(8,128)(2,1)}, u32[]{:S(2)}, u32[]{:S(2)}) collective-permute-start(bf16[2,1536,256]{2,1,0:T(8,128)(2,1)} %get-tuple-element.65.rest_0_.rest_1_), channel_id=1, source_target_pairs={{0,4},{1,13},{4,8},{5,1},{8,12},{9,5},{12,0},{13,9},{2,6},{3,15},{... | collective-permute-start | bytes 4718600 | tf_op jit(solution)/shard_map/ppermute | solution.py:23
  93.8 2.3 %collective-permute-start.28 = (bf16[2,1536,256]{2,1,0:T(8,128)(2,1)S(1)}, bf16[2,1536,256]{2,1,0:T(8,128)(2,1)}, u32[]{:S(2)}, u32[]{:S(2)}) collective-permute-start(bf16[2,1536,256]{2,1,0:T(8,128)(2,1)S(1)} %collective-permute-done.24.rest_2_), channel_id=1, source_target_pairs={{0,4},{1,13},{4,8},{5,1},{8,12},{9,5},{12,0},{13,9},{2,6},{3,15},{... | collective-permute-start | bytes 4718600 | tf_op jit(solution)/shard_map/ppermute | solution.py:23
  96.1 30.6 %collective-permute-done.25.rest_3_ = bf16[2,1536,256]{2,1,0:T(8,128)(2,1)S(1)} collective-permute-done((bf16[2,1536,256]{2,1,0:T(8,128)(2,1)}, bf16[2,1536,256]{2,1,0:T(8,128)(2,1)S(1)}, u32[]{:S(2)}, u32[]{:S(2)}) %collective-permute-start.25) | collective-permute-done | bytes 1572896 | tf_op jit(solution)/shard_map/ppermute | solution.py:32
  127.6 2.1 %collective-permute-start.29 = (bf16[2,1536,256]{2,1,0:T(8,128)(2,1)}, bf16[2,1536,256]{2,1,0:T(8,128)(2,1)}, u32[]{:S(2)}, u32[]{:S(2)}) collective-permute-start(bf16[2,1536,256]{2,1,0:T(8,128)(2,1)} %collective-permute-done.28.rest_6_), channel_id=1, source_target_pairs={{0,1},{1,0},{2,3},{3,2},{4,5},{5,4},{6,7},{7,6},{8,9},{9,8},{10,11... | collective-permute-start | bytes 4718600 | tf_op jit(solution)/shard_map/ppermute | solution.py:32
  132.3 2.1 %collective-permute-start.35 = (bf16[2,1536,256]{2,1,0:T(8,128)(2,1)}, bf16[2,1536,256]{2,1,0:T(8,128)(2,1)}, u32[]{:S(2)}, u32[]{:S(2)}) collective-permute-start(bf16[2,1536,256]{2,1,0:T(8,128)(2,1)} %collective-permute-done.27.rest_4_), channel_id=1, source_target_pairs={{0,4},{1,13},{4,8},{5,1},{8,12},{9,5},{12,0},{13,9},{2,6},{3,15},{... | collective-permute-start | bytes 4718600 | tf_op jit(solution)/shard_map/ppermute | solution.py:23
  136.4 13.1 %shard_map.60 = (f32[512,8192]{1,0:T(8,128)}, f32[8,128]{1,0:T(8,128)}, bf16[512,1536]{1,0:T(8,128)(2,1)}) custom-call(s32[8]{0:T(128)} %stack.164.ids_ref, f32[1]{0:T(128)} %bitcast.2.scale_ref, bf16[2,1536,256]{2,1,0:T(8,128)(2,1)} %get-tuple-element.65.rest_0_.rest_1_, bf16[2,1536,256]{2,1,0:T(8,128)(2,1)} %get-tuple-element.65.rest_0_.rest_1_, ...), custom_call_target="tpu_custom_call" | custom-call | flops 1150000000 | bytes 1000000 | tf_op jit(solution)/shard_map/pallas_call | solution.py:261
  149.6 17.5 %collective-permute-done.33.rest_1_ = bf16[2,1536,256]{2,1,0:T(8,128)(2,1)S(1)} collective-permute-done((bf16[2,1536,256]{2,1,0:T(8,128)(2,1)}, bf16[2,1536,256]{2,1,0:T(8,128)(2,1)S(1)}, u32[]{:S(2)}, u32[]{:S(2)}) %collective-permute-start.33) | collective-permute-done | bytes 1572896 | tf_op jit(solution)/shard_map/ppermute | solution.py:32
  174.2 2.1 %collective-permute-done.38.rest_6_ = bf16[2,1536,256]{2,1,0:T(8,128)(2,1)} collective-permute-done((bf16[2,1536,256]{2,1,0:T(8,128)(2,1)S(1)}, bf16[2,1536,256]{2,1,0:T(8,128)(2,1)}, u32[]{:S(2)}, u32[]{:S(2)}) %collective-permute-start.38) | collective-permute-done | bytes 1572896 | tf_op jit(solution)/shard_map/ppermute | solution.py:32
  176.2 10.1 %shard_map.61 = (f32[512,8192]{1,0:T(8,128)}, f32[8,128]{1,0:T(8,128)}) custom-call(s32[6]{0:T(128)} %stack.203.ids_ref, f32[1]{0:T(128)} %bitcast.2.scale_ref, bf16[512,1536]{1,0:T(8,128)(2,1)} %get-tuple-element.70.rest_0_, bf16[2,1536,256]{2,1,0:T(8,128)(2,1)} %copy-done, ...), custom_call_target="tpu_custom_call", output_to_operand_aliasing={{0}: (10, {})} | custom-call | flops 1150000000 | bytes 1000000 | tf_op jit(solution)/shard_map/pallas_call | solution.py:261
  187.6 2.5 %collective-permute-done.39.rest_3_ = bf16[2,512,256]{2,1,0:T(8,128)(2,1)S(1)} collective-permute-done((bf16[2,512,256]{2,1,0:T(8,128)(2,1)}, bf16[2,512,256]{2,1,0:T(8,128)(2,1)S(1)}, u32[]{:S(2)}, u32[]{:S(2)}) %collective-permute-start.39) | collective-permute-done | bytes 524320 | tf_op jit(solution)/shard_map/ppermute | solution.py:32
  191.3 6.3 %shard_map.62 = (f32[512,8192]{1,0:T(8,128)}, f32[8,128]{1,0:T(8,128)}) custom-call(s32[2]{0:T(128)} %pad_add_fusion.ids_ref, f32[1]{0:T(128)} %bitcast.2.scale_ref, bf16[512,1536]{1,0:T(8,128)(2,1)} %get-tuple-element.70.rest_0_, bf16[2,512,256]{2,1,0:T(8,128)(2,1)} %collective-permute-done.32.rest_1_, ...), custom_call_target="tpu_custom_call", output_to_operand_aliasing={{0}: (8, {})} | custom-call | flops 1150000000 | bytes 1000000 | tf_op jit(solution)/shard_map/pallas_call | solution.py:261
  (140 shorter events, 45.3 us)
Async XLA Ops:
  1.7 7.3 %collective-permute-start = (bf16[16,3200]{1,0:T(8,128)(2,1)S(1)}, bf16[16,3200]{1,0:T(8,128)(2,1)S(1)}, u32[]{:S(2)}, u32[]{:S(2)}) collective-permute-start(bf16[16,3200]{1,0:T(8,128)(2,1)S(1)} %get-tuple-element.86), channel_id=1, source_target_pairs={{0,18},{18,0},{2,16},{16,2},{1,19},{19,1},{3,17},{17,3},{4,22},{22... | collective-permute-start | bytes 307208 | tf_op jit(solution)/shard_map/ppermute | solution.py:36
  11.8 8.2 %collective-permute-start.4 = (bf16[2,16,3200]{2,1,0:T(8,128)(2,1)S(1)}, bf16[2,16,3200]{2,1,0:T(8,128)(2,1)S(1)}, u32[]{:S(2)}, u32[]{:S(2)}) collective-permute-start(bf16[2,16,3200]{2,1,0:T(8,128)(2,1)S(1)} %pad_maximum_fusion), channel_id=1, source_target_pairs={{0,96},{1,33},{32,0},{33,65},{64,32},{65,97},{96,64},{97,1},{2,98}... | collective-permute-start | bytes 614408 | tf_op jit(solution)/shard_map/ppermute | solution.py:28
  11.8 10.4 %collective-permute-start.6 = (bf16[2,16,3200]{2,1,0:T(8,128)(2,1)S(1)}, bf16[2,16,3200]{2,1,0:T(8,128)(2,1)S(1)}, u32[]{:S(2)}, u32[]{:S(2)}) collective-permute-start(bf16[2,16,3200]{2,1,0:T(8,128)(2,1)S(1)} %pad_maximum_fusion), channel_id=1, source_target_pairs={{0,64},{32,96},{64,0},{96,32},{1,65},{33,97},{65,1},{97,33},{2,66}... | collective-permute-start | bytes 614408 | tf_op jit(solution)/shard_map/ppermute | solution.py:355
  13.5 10.7 %collective-permute-start.1 = (bf16[2,16,3200]{2,1,0:T(8,128)(2,1)S(1)}, bf16[2,16,3200]{2,1,0:T(8,128)(2,1)S(1)}, u32[]{:S(2)}, u32[]{:S(2)}) collective-permute-start(bf16[2,16,3200]{2,1,0:T(8,128)(2,1)S(1)} %pad_maximum_fusion), channel_id=1, source_target_pairs={{0,1},{1,0},{2,3},{3,2},{4,5},{5,4},{6,7},{7,6},{8,9},{9,8},{10,11... | collective-permute-start | bytes 614408 | tf_op jit(solution)/shard_map/ppermute | solution.py:32
  15.5 8.6 %collective-permute-start.3 = (bf16[2,16,3200]{2,1,0:T(8,128)(2,1)S(1)}, bf16[2,16,3200]{2,1,0:T(8,128)(2,1)S(1)}, u32[]{:S(2)}, u32[]{:S(2)}) collective-permute-start(bf16[2,16,3200]{2,1,0:T(8,128)(2,1)S(1)} %collective-permute-done.2), channel_id=1, source_target_pairs={{0,1},{1,0},{2,3},{3,2},{4,5},{5,4},{6,7},{7,6},{8,9},{9,8},{10,11... | collective-permute-start | bytes 614408 | tf_op jit(solution)/shard_map/ppermute | solution.py:32
  29.6 14.8 %collective-permute-start.8 = (bf16[2,96,1536]{2,1,0:T(8,128)(2,1)}, bf16[2,96,1536]{2,1,0:T(8,128)(2,1)S(1)}, u32[]{:S(2)}, u32[]{:S(2)}) collective-permute-start(bf16[2,96,1536]{2,1,0:T(8,128)(2,1)} %get-tuple-element.45.rest_0_), channel_id=1, source_target_pairs={{0,2},{2,0},{1,3},{3,1},{4,6},{6,4},{5,7},{7,5},{8,10},{10,8},{9,1... | collective-permute-start | bytes 1769480 | tf_op jit(solution)/shard_map/ppermute | solution.py:32
  29.7 14.7 %collective-permute-start.9 = (bf16[2,96,1536]{2,1,0:T(8,128)(2,1)}, bf16[2,96,1536]{2,1,0:T(8,128)(2,1)S(1)}, u32[]{:S(2)}, u32[]{:S(2)}) collective-permute-start(bf16[2,96,1536]{2,1,0:T(8,128)(2,1)} %get-tuple-element.45.rest_0_), channel_id=1, source_target_pairs={{0,4},{1,13},{4,8},{5,1},{8,12},{9,5},{12,0},{13,9},{2,6},{3,15},{... | collective-permute-start | bytes 1769480 | tf_op jit(solution)/shard_map/ppermute | solution.py:23
  32.3 13.6 %collective-permute-start.12 = (bf16[2,96,1536]{2,1,0:T(8,128)(2,1)}, bf16[2,96,1536]{2,1,0:T(8,128)(2,1)S(1)}, u32[]{:S(2)}, u32[]{:S(2)}) collective-permute-start(bf16[2,96,1536]{2,1,0:T(8,128)(2,1)} %get-tuple-element.46.rest_1_), channel_id=1, source_target_pairs={{0,4},{1,13},{4,8},{5,1},{8,12},{9,5},{12,0},{13,9},{2,6},{3,15},{... | collective-permute-start | bytes 1769480 | tf_op jit(solution)/shard_map/ppermute | solution.py:23
  47.8 13.7 %collective-permute-start.10 = (bf16[2,96,1536]{2,1,0:T(8,128)(2,1)S(1)}, bf16[2,96,1536]{2,1,0:T(8,128)(2,1)S(1)}, u32[]{:S(2)}, u32[]{:S(2)}) collective-permute-start(bf16[2,96,1536]{2,1,0:T(8,128)(2,1)S(1)} %collective-permute-done.9.rest_2_), channel_id=1, source_target_pairs={{0,4},{1,13},{4,8},{5,1},{8,12},{9,5},{12,0},{13,9},{2,6},{3,15},{... | collective-permute-start | bytes 1769480 | tf_op jit(solution)/shard_map/ppermute | solution.py:23
  49.0 14.8 %collective-permute-start.16 = (bf16[2,96,1536]{2,1,0:T(8,128)(2,1)S(1)}, bf16[2,96,1536]{2,1,0:T(8,128)(2,1)S(1)}, u32[]{:S(2)}, u32[]{:S(2)}) collective-permute-start(bf16[2,96,1536]{2,1,0:T(8,128)(2,1)S(1)} %collective-permute-done.9.rest_2_), channel_id=1, source_target_pairs={{0,2},{2,0},{1,3},{3,1},{4,6},{6,4},{5,7},{7,5},{8,10},{10,8},{9,1... | collective-permute-start | bytes 1769480 | tf_op jit(solution)/shard_map/ppermute | solution.py:32
  50.7 13.7 %collective-permute-start.18 = (bf16[2,96,1536]{2,1,0:T(8,128)(2,1)}, bf16[2,96,1536]{2,1,0:T(8,128)(2,1)S(1)}, u32[]{:S(2)}, u32[]{:S(2)}) collective-permute-start(bf16[2,96,1536]{2,1,0:T(8,128)(2,1)} %collective-permute-done.11.rest_1_), channel_id=1, source_target_pairs={{0,4},{1,13},{4,8},{5,1},{8,12},{9,5},{12,0},{13,9},{2,6},{3,15},{... | collective-permute-start | bytes 1769480 | tf_op jit(solution)/shard_map/ppermute | solution.py:23
  66.0 14.4 %collective-permute-start.17 = (bf16[2,64,1536]{2,1,0:T(8,128)(2,1)}, bf16[2,64,1536]{2,1,0:T(8,128)(2,1)}, u32[]{:S(2)}, u32[]{:S(2)}) collective-permute-start(bf16[2,64,1536]{2,1,0:T(8,128)(2,1)} %slice.13), channel_id=1, source_target_pairs={{0,4},{1,13},{4,8},{5,1},{8,12},{9,5},{12,0},{13,9},{2,6},{3,15},{... | collective-permute-start | bytes 1179656 | tf_op jit(solution)/shard_map/ppermute | solution.py:23
  67.5 12.9 %collective-permute-start.15 = (bf16[2,32,1536]{2,1,0:T(8,128)(2,1)}, bf16[2,32,1536]{2,1,0:T(8,128)(2,1)}, u32[]{:S(2)}, u32[]{:S(2)}) collective-permute-start(bf16[2,32,1536]{2,1,0:T(8,128)(2,1)} %slice.12), channel_id=1, source_target_pairs={{0,2},{2,0},{1,3},{3,1},{4,6},{6,4},{5,7},{7,5},{8,10},{10,8},{9,1... | collective-permute-start | bytes 589832 | tf_op jit(solution)/shard_map/ppermute | solution.py:32
  90.5 36.2 %collective-permute-start.25 = (bf16[2,1536,256]{2,1,0:T(8,128)(2,1)}, bf16[2,1536,256]{2,1,0:T(8,128)(2,1)S(1)}, u32[]{:S(2)}, u32[]{:S(2)}) collective-permute-start(bf16[2,1536,256]{2,1,0:T(8,128)(2,1)} %get-tuple-element.65.rest_0_.rest_1_), channel_id=1, source_target_pairs={{0,2},{2,0},{1,3},{3,1},{4,6},{6,4},{5,7},{7,5},{8,10},{10,8},{9,1... | collective-permute-start | bytes 4718600 | tf_op jit(solution)/shard_map/ppermute | solution.py:32
  90.5 36.1 %collective-permute-start.26 = (bf16[2,1536,256]{2,1,0:T(8,128)(2,1)}, bf16[2,1536,256]{2,1,0:T(8,128)(2,1)}, u32[]{:S(2)}, u32[]{:S(2)}) collective-permute-start(bf16[2,1536,256]{2,1,0:T(8,128)(2,1)} %get-tuple-element.65.rest_0_.rest_1_), channel_id=1, source_target_pairs={{0,4},{1,13},{4,8},{5,1},{8,12},{9,5},{12,0},{13,9},{2,6},{3,15},{... | collective-permute-start | bytes 4718600 | tf_op jit(solution)/shard_map/ppermute | solution.py:23
  93.8 33.8 %collective-permute-start.28 = (bf16[2,1536,256]{2,1,0:T(8,128)(2,1)S(1)}, bf16[2,1536,256]{2,1,0:T(8,128)(2,1)}, u32[]{:S(2)}, u32[]{:S(2)}) collective-permute-start(bf16[2,1536,256]{2,1,0:T(8,128)(2,1)S(1)} %collective-permute-done.24.rest_2_), channel_id=1, source_target_pairs={{0,4},{1,13},{4,8},{5,1},{8,12},{9,5},{12,0},{13,9},{2,6},{3,15},{... | collective-permute-start | bytes 4718600 | tf_op jit(solution)/shard_map/ppermute | solution.py:23
  127.5 8.9 %collective-permute-start.30 = (bf16[2,1536,256]{2,1,0:T(8,128)(2,1)}, bf16[2,1536,256]{2,1,0:T(8,128)(2,1)}, u32[]{:S(2)}, u32[]{:S(2)}) collective-permute-start(bf16[2,1536,256]{2,1,0:T(8,128)(2,1)} %collective-permute-done.26.rest_5_), channel_id=1, source_target_pairs={{0,1},{1,0},{2,3},{3,2},{4,5},{5,4},{6,7},{7,6},{8,9},{9,8},{10,11... | collective-permute-start | bytes 4718600 | tf_op jit(solution)/shard_map/ppermute | solution.py:32
  127.6 8.8 %collective-permute-start.29 = (bf16[2,1536,256]{2,1,0:T(8,128)(2,1)}, bf16[2,1536,256]{2,1,0:T(8,128)(2,1)}, u32[]{:S(2)}, u32[]{:S(2)}) collective-permute-start(bf16[2,1536,256]{2,1,0:T(8,128)(2,1)} %collective-permute-done.28.rest_6_), channel_id=1, source_target_pairs={{0,1},{1,0},{2,3},{3,2},{4,5},{5,4},{6,7},{7,6},{8,9},{9,8},{10,11... | collective-permute-start | bytes 4718600 | tf_op jit(solution)/shard_map/ppermute | solution.py:32
  129.8 19.8 %collective-permute-start.31 = (bf16[2,1536,256]{2,1,0:T(8,128)(2,1)}, bf16[2,1536,256]{2,1,0:T(8,128)(2,1)S(1)}, u32[]{:S(2)}, u32[]{:S(2)}) collective-permute-start(bf16[2,1536,256]{2,1,0:T(8,128)(2,1)} %collective-permute-done.26.rest_5_), channel_id=1, source_target_pairs={{0,4},{1,13},{4,8},{5,1},{8,12},{9,5},{12,0},{13,9},{2,6},{3,15},{... | collective-permute-start | bytes 4718600 | tf_op jit(solution)/shard_map/ppermute | solution.py:23
  130.6 36.5 %collective-permute-start.33 = (bf16[2,1536,256]{2,1,0:T(8,128)(2,1)}, bf16[2,1536,256]{2,1,0:T(8,128)(2,1)S(1)}, u32[]{:S(2)}, u32[]{:S(2)}) collective-permute-start(bf16[2,1536,256]{2,1,0:T(8,128)(2,1)} %collective-permute-done.26.rest_5_), channel_id=1, source_target_pairs={{0,2},{2,0},{1,3},{3,1},{4,6},{6,4},{5,7},{7,5},{8,10},{10,8},{9,1... | collective-permute-start | bytes 4718600 | tf_op jit(solution)/shard_map/ppermute | solution.py:32
  132.3 34.8 %collective-permute-start.35 = (bf16[2,1536,256]{2,1,0:T(8,128)(2,1)}, bf16[2,1536,256]{2,1,0:T(8,128)(2,1)}, u32[]{:S(2)}, u32[]{:S(2)}) collective-permute-start(bf16[2,1536,256]{2,1,0:T(8,128)(2,1)} %collective-permute-done.27.rest_4_), channel_id=1, source_target_pairs={{0,4},{1,13},{4,8},{5,1},{8,12},{9,5},{12,0},{13,9},{2,6},{3,15},{... | collective-permute-start | bytes 4718600 | tf_op jit(solution)/shard_map/ppermute | solution.py:23
  168.6 7.7 %collective-permute-start.38 = (bf16[2,1536,256]{2,1,0:T(8,128)(2,1)S(1)}, bf16[2,1536,256]{2,1,0:T(8,128)(2,1)}, u32[]{:S(2)}, u32[]{:S(2)}) collective-permute-start(bf16[2,1536,256]{2,1,0:T(8,128)(2,1)S(1)} %collective-permute-done.31.rest_5_), channel_id=1, source_target_pairs={{0,1},{1,0},{2,3},{3,2},{4,5},{5,4},{6,7},{7,6},{8,9},{9,8},{10,11... | collective-permute-start | bytes 4718600 | tf_op jit(solution)/shard_map/ppermute | solution.py:32
  170.1 16.3 %collective-permute-start.34 = (bf16[2,1024,256]{2,1,0:T(8,128)(2,1)}, bf16[2,1024,256]{2,1,0:T(8,128)(2,1)}, u32[]{:S(2)}, u32[]{:S(2)}) collective-permute-start(bf16[2,1024,256]{2,1,0:T(8,128)(2,1)} %slice.15), channel_id=1, source_target_pairs={{0,4},{1,13},{4,8},{5,1},{8,12},{9,5},{12,0},{13,9},{2,6},{3,15},{... | collective-permute-start | bytes 3145736 | tf_op jit(solution)/shard_map/ppermute | solution.py:23
  171.0 15.4 %collective-permute-start.32 = (bf16[2,512,256]{2,1,0:T(8,128)(2,1)}, bf16[2,512,256]{2,1,0:T(8,128)(2,1)}, u32[]{:S(2)}, u32[]{:S(2)}) collective-permute-start(bf16[2,512,256]{2,1,0:T(8,128)(2,1)} %slice.14), channel_id=1, source_target_pairs={{0,2},{2,0},{1,3},{3,1},{4,6},{6,4},{5,7},{7,5},{8,10},{10,8},{9,1... | collective-permute-start | bytes 1572872 | tf_op jit(solution)/shard_map/ppermute | solution.py:32
  (43 other events, 285.2 us)
where the time goes:
time: 198 us
  waiting for transfers between devices  67.9 us (34%)
  Pallas kernels  65.4 us (33%)
  starting transfers between devices  48.4 us (24%)
  local copies, waits for them, and re-layouts  10.8 us (5%)
  other arithmetic  4.08 us (2%)
    ppermute x27, waiting for transfers between devices, swap(): return lax.ppermute(a, axis, [(0, 1), (1, 0)])  63.1 us
    pallas_call x4, Pallas kernels, ffn(): pl.pallas_call(functools.partial(ffn_kernel, sources, len(arrays), len(ol...  31.9 us
    pallas_call x3, Pallas kernels, gram(): pl.pallas_call(functools.partial(gram_kernel, sources, len(arrays), first...  29.5 us
    ppermute x27, starting transfers between devices, swap(): return lax.ppermute(a, axis, [(0, 1), (1, 0)])  26 us
    ppermute x11, starting transfers between devices, ring_hop(): return lax.ppermute(a, (axis, 'c'), pairs)  16 us
    ppermute x1, starting transfers between devices, far_swap(): return lax.ppermute(a, ('h', 'l'), [(0, 3), (3, 0), (1, 2), (2, 1)])  4.67 us
    pallas_call x1, Pallas kernels, select(): pl.pallas_call(functools.partial(select_kernel, len(blocks), width), out_...  3.97 us
  transfers between devices with their start and end apart: 41, of which 13 were waited for; matrix products, arithmetic and copies ran while one was open for 5% of the time, Pallas kernels for 25%

commit v1 on v0

--- a/solution.py
+++ b/solution.py
@@ -137,7 +137,8 @@
             weight_copies.append(
                 pltpu.make_async_copy(src.at[:, cols], dst.at[:, cols], weight_sems.at[2 * q + j])
             )
-    for copy in weight_copies[:2] + copies + weight_copies[2:]:
+    late = weight_copies[2:] if len(blocks) > 2 else []
+    for copy in weight_copies[:2] + copies + ([] if late else weight_copies[2:]):
         copy.start()
     for copy in copies:
         copy.wait()
@@ -145,6 +146,9 @@
     for q in range(2):
         weight_copies[2 * q].wait()
         weight_copies[2 * q + 1].wait()
+        if q == 0:
+            for copy in late:
+                copy.start()
         cols = slice(q * half, (q + 1) * half)
         gate = jnp.dot(rows[...], gate_held[:, cols], preferred_element_type=jnp.float32)
         up = jnp.dot(rows[...], up_held[:, cols], preferred_element_type=jnp.float32)
@@ -303,19 +307,15 @@
 
     def first(self, token):
         beside, near, near_twin = self.moved
-        beside, near, token = lax.optimization_barrier((beside, near, token))
-        self.moved = (beside, near, near_twin)
-        return token
-
-    def second(self):
-        beside, near, near_twin = self.moved
-        near_beside = swap(near, "l")
-        far = ring_hop(near, "x")
+        near, token = tie(near, token)
+        near_beside, far = swap(near, "l"), ring_hop(near, "x")
+        beside, near_twin, token = lax.optimization_barrier((beside, near_twin, token))
         (twin,) = self.keep([beside], "o", 1, 0)
         beside_near = ring_hop(twin, "x")
         self.keep([near], "m", 0, 0)
         self.keep([near_twin], "m", 0, 1)
         self.moved = (far, near_beside, beside_near)
+        return token
 
     def third(self, token):
         far, near_beside, beside_near = self.moved
@@ -392,7 +392,6 @@
     rows.open(pair, twin)
     hidden, token = hidden_of([("o", 0)], token)
     token = rows.first(token)
-    rows.second()
     hidden, token = hidden_of([("o", 1), ("m", 0), ("p", 0)], token, hidden)
     token = rows.third(token)
     hidden, token = hidden_of([("m", 1), ("p", 1), ("f", 0)], token, hidden)
@@ -407,7 +406,6 @@
     panels = Spread()
     panels.open(hidden)
     token = panels.first(token)
-    panels.second()
     own = hidden
     out, token, own = part([("o", 0), ("o", 1), ("m", 0), ("p", 0)], token)
     token = panels.third(token)

time: 198 us -> 196 us (0.990)
  starting transfers between devices: 48.4 us -> 41 us
  waiting for transfers between devices: 67.9 us -> 74.2 us
    ppermute x11, waiting for transfers between devices: 0.03 us -> 14.5 us  [ring_hop(): return lax.ppermute(a, (axis, 'c'), pairs)]
    ppermute x27, waiting for transfers between devices: 63.1 us -> 54.9 us  [swap(): return lax.ppermute(a, axis, [(0, 1), (1, 0)])]
    ppermute x27, starting transfers between devices: 26 us -> 20.2 us  [swap(): return lax.ppermute(a, axis, [(0, 1), (1, 0)])]
  transfers between devices with their start and end apart: 41 -> 41, of which waited for: 13 -> 15; matrix products, arithmetic and copies ran while one was open for 5% -> 5% of each run, Pallas kernels for 25% -> 24%
where the time goes in v1:
time: 196 us
  waiting for transfers between devices  74.2 us (38%)
  Pallas kernels  64.5 us (33%)
  starting transfers between devices  41 us (21%)
  local copies, waits for them, and re-layouts  10.6 us (5%)
  other arithmetic  4.08 us (2%)
    ppermute x27, waiting for transfers between devices, swap(): return lax.ppermute(a, axis, [(0, 1), (1, 0)])  54.9 us
    pallas_call x4, Pallas kernels, ffn(): pl.pallas_call(functools.partial(ffn_kernel, sources, len(arrays), len(ol...  31 us
    pallas_call x3, Pallas kernels, gram(): pl.pallas_call(functools.partial(gram_kernel, sources, len(arrays), first...  29.5 us
    ppermute x27, starting transfers between devices, swap(): return lax.ppermute(a, axis, [(0, 1), (1, 0)])  20.2 us
    ppermute x11, waiting for transfers between devices, ring_hop(): return lax.ppermute(a, (axis, 'c'), pairs)  14.5 us
    ppermute x11, starting transfers between devices, ring_hop(): return lax.ppermute(a, (axis, 'c'), pairs)  14.5 us
    ppermute x1, starting transfers between devices, far_swap(): return lax.ppermute(a, ('h', 'l'), [(0, 3), (3, 0), (1, 2), (2, 1)])  4.67 us
    pallas_call x1, Pallas kernels, select(): pl.pallas_call(functools.partial(select_kernel, len(blocks), width), out_...  3.96 us
  transfers between devices with their start and end apart: 41, of which 15 were waited for; matrix products, arithmetic and copies ran while one was open for 5% of the time, Pallas kernels for 24%

profile of v1, /device:TPU:1, one launch (start us, length us, event | category | flops | bytes accessed | tf_op | source)
XLA Modules:
  0.0 195.7 jit_solution(13419367118877099037)
XLA Ops:
  1.7 4.7 %collective-permute-start = (bf16[16,3200]{1,0:T(8,128)(2,1)S(1)}, bf16[16,3200]{1,0:T(8,128)(2,1)S(1)}, u32[]{:S(2)}, u32[]{:S(2)}) collective-permute-start(bf16[16,3200]{1,0:T(8,128)(2,1)S(1)} %get-tuple-element.94), channel_id=1, source_target_pairs={{0,18},{18,0},{2,16},{16,2},{1,19},{19,1},{3,17},{17,3},{4,22},{22... | collective-permute-start | bytes 307208 | tf_op jit(solution)/shard_map/ppermute | solution.py:36
  6.4 2.6 %collective-permute-done = bf16[16,3200]{1,0:T(8,128)(2,1)S(1)} collective-permute-done((bf16[16,3200]{1,0:T(8,128)(2,1)S(1)}, bf16[16,3200]{1,0:T(8,128)(2,1)S(1)}, u32[]{:S(2)}, u32[]{:S(2)}) %collective-permute-start) | collective-permute-done | bytes 102432 | tf_op jit(solution)/shard_map/ppermute | solution.py:36
  9.0 2.8 %collective-permute-start.2 = (bf16[2,16,3200]{2,1,0:T(8,128)(2,1)S(1)}, bf16[2,16,3200]{2,1,0:T(8,128)(2,1)S(1)}, u32[]{:S(2)}, u32[]{:S(2)}) collective-permute-start(bf16[2,16,3200]{2,1,0:T(8,128)(2,1)S(1)} %pad_maximum_fusion), channel_id=1, source_target_pairs={{0,32},{1,97},{32,64},{33,1},{64,96},{65,33},{96,0},{97,65},{2,34}... | collective-permute-start | bytes 614408 | tf_op jit(solution)/shard_map/ppermute | solution.py:23
  13.5 2.1 %collective-permute-start.1 = (bf16[2,16,3200]{2,1,0:T(8,128)(2,1)S(1)}, bf16[2,16,3200]{2,1,0:T(8,128)(2,1)S(1)}, u32[]{:S(2)}, u32[]{:S(2)}) collective-permute-start(bf16[2,16,3200]{2,1,0:T(8,128)(2,1)S(1)} %pad_maximum_fusion), channel_id=1, source_target_pairs={{0,1},{1,0},{2,3},{3,2},{4,5},{5,4},{6,7},{7,6},{8,9},{9,8},{10,11... | collective-permute-start | bytes 614408 | tf_op jit(solution)/shard_map/ppermute | solution.py:32
  15.5 3.1 %collective-permute-start.3 = (bf16[2,16,3200]{2,1,0:T(8,128)(2,1)S(1)}, bf16[2,16,3200]{2,1,0:T(8,128)(2,1)S(1)}, u32[]{:S(2)}, u32[]{:S(2)}) collective-permute-start(bf16[2,16,3200]{2,1,0:T(8,128)(2,1)S(1)} %collective-permute-done.2), channel_id=1, source_target_pairs={{0,1},{1,0},{2,3},{3,2},{4,5},{5,4},{6,7},{7,6},{8,9},{9,8},{10,11... | collective-permute-start | bytes 614408 | tf_op jit(solution)/shard_map/ppermute | solution.py:32
  25.6 4.0 %shard_map.55 = (bf16[2,96,1536]{2,1,0:T(8,128)(2,1)}, bf16[2,96,1536]{2,1,0:T(8,128)(2,1)}) custom-call(s32[1]{0:T(128)} %bitcast.13.expert_ref, f32[8,256]{1,0:T(8,128)} %broadcast_in_dim.18.base_ref, bf16[32,3200]{1,0:T(8,128)(2,1)} %bitcast.64, bf16[32,3200]{1,0:T(8,128)(2,1)} %bitcast.69, bf16[32,3200]{1,0:T(8,128)(2,1)} %bitcast.66, ...), custom_call_target="tpu_custom_call" | custom-call | flops 3449999872 | bytes 1000000 | tf_op jit(solution)/shard_map/pallas_call | solution.py:90
  29.6 2.5 %collective-permute-start.8 = (bf16[2,96,1536]{2,1,0:T(8,128)(2,1)}, bf16[2,96,1536]{2,1,0:T(8,128)(2,1)S(1)}, u32[]{:S(2)}, u32[]{:S(2)}) collective-permute-start(bf16[2,96,1536]{2,1,0:T(8,128)(2,1)} %get-tuple-element.49.rest_0_), channel_id=1, source_target_pairs={{0,4},{1,13},{4,8},{5,1},{8,12},{9,5},{12,0},{13,9},{2,6},{3,15},{... | collective-permute-start | bytes 1769480 | tf_op jit(solution)/shard_map/ppermute | solution.py:23
  33.9 6.3 %shard_map.56 = (bf16[2,1536,256]{2,1,0:T(8,128)(2,1)}, f32[8,128]{1,0:T(8,128)}) custom-call(s32[2]{0:T(128)} %pad_add_fusion.2.offsets_ref, bf16[2,96,1536]{2,1,0:T(8,128)(2,1)} %get-tuple-element.49.rest_0_, bf16[2,96,1536]{2,1,0:T(8,128)(2,1)} %get-tuple-element.50.rest_1_, bf16[3072,512]{1,0:T(8,128)(2,1)} %bitcast.56, bf16[3072,512]{1,0:T(8,128)(2,1)} %bitcast.60, ...), custom_call_target="tpu_custom_call" | custom-call | flops 1150000000 | bytes 1000000 | tf_op jit(solution)/shard_map/pallas_call | solution.py:191
  40.2 7.2 %collective-permute-done.10.rest_0_ = bf16[2,96,1536]{2,1,0:T(8,128)(2,1)S(1)} collective-permute-done((bf16[2,96,1536]{2,1,0:T(8,128)(2,1)}, bf16[2,96,1536]{2,1,0:T(8,128)(2,1)S(1)}, u32[]{:S(2)}, u32[]{:S(2)}) %collective-permute-start.10) | collective-permute-done | bytes 589856 | tf_op jit(solution)/shard_map/ppermute | solution.py:32
  51.4 9.1 %shard_map.57 = (bf16[2,1536,256]{2,1,0:T(8,128)(2,1)}, f32[8,128]{1,0:T(8,128)}) custom-call(s32[6]{0:T(128)} %stack.189.offsets_ref, bf16[2,96,1536]{2,1,0:T(8,128)(2,1)} %copy-done.8, bf16[2,96,1536]{2,1,0:T(8,128)(2,1)} %collective-permute-done.12.rest_1_, bf16[2,96,1536]{2,1,0:T(8,128)(2,1)} %copy-done.7, ...), custom_call_target="tpu_custom_call", output_to_operand_aliasing={{0}: (10, {})} | custom-call | flops 1150000000 | bytes 1000000 | tf_op jit(solution)/shard_map/pallas_call | solution.py:191
  60.5 3.8 %collective-permute-done.16.rest_0_ = bf16[2,96,1536]{2,1,0:T(8,128)(2,1)S(1)} collective-permute-done((bf16[2,96,1536]{2,1,0:T(8,128)(2,1)S(1)}, bf16[2,96,1536]{2,1,0:T(8,128)(2,1)S(1)}, u32[]{:S(2)}, u32[]{:S(2)}) %collective-permute-start.16) | collective-permute-done | bytes 589856 | tf_op jit(solution)/shard_map/ppermute | solution.py:32
  69.6 9.1 %shard_map.58 = (bf16[2,1536,256]{2,1,0:T(8,128)(2,1)}, f32[8,128]{1,0:T(8,128)}) custom-call(s32[6]{0:T(128)} %stack.196.offsets_ref, bf16[2,96,1536]{2,1,0:T(8,128)(2,1)} %copy-done.2, bf16[2,96,1536]{2,1,0:T(8,128)(2,1)} %copy-done.10, bf16[2,96,1536]{2,1,0:T(8,128)(2,1)} %copy-done.13, ...), custom_call_target="tpu_custom_call", output_to_operand_aliasing={{0}: (10, {})} | custom-call | flops 1150000000 | bytes 1000000 | tf_op jit(solution)/shard_map/pallas_call | solution.py:191
  82.0 6.5 %shard_map.59 = (bf16[2,1536,256]{2,1,0:T(8,128)(2,1)}, f32[8,128]{1,0:T(8,128)}) custom-call(s32[2]{0:T(128)} %pad_add_fusion.1.offsets_ref, bf16[2,32,1536]{2,1,0:T(8,128)(2,1)} %collective-permute-done.15.rest_0_, bf16[2,64,1536]{2,1,0:T(8,128)(2,1)} %collective-permute-done.17.rest_1_, ...), custom_call_target="tpu_custom_call", output_to_operand_aliasing={{0}: (8, {})} | custom-call | flops 1150000000 | bytes 1000000 | tf_op jit(solution)/shard_map/pallas_call | solution.py:191
  89.0 2.1 %collective-permute-start.27 = (bf16[2,1536,256]{2,1,0:T(8,128)(2,1)}, bf16[2,1536,256]{2,1,0:T(8,128)(2,1)}, u32[]{:S(2)}, u32[]{:S(2)}) collective-permute-start(bf16[2,1536,256]{2,1,0:T(8,128)(2,1)} %get-tuple-element.71.rest_0_.rest_1_), channel_id=1, source_target_pairs={{0,4},{1,13},{4,8},{5,1},{8,12},{9,5},{12,0},{13,9},{2,6},{3,15},{... | collective-permute-start | bytes 4718600 | tf_op jit(solution)/shard_map/ppermute | solution.py:23
  91.1 1.7 collective-permute-start.25
  94.4 14.5 %collective-permute-done.27.rest_5_ = bf16[2,1536,256]{2,1,0:T(8,128)(2,1)} collective-permute-done((bf16[2,1536,256]{2,1,0:T(8,128)(2,1)}, bf16[2,1536,256]{2,1,0:T(8,128)(2,1)}, u32[]{:S(2)}, u32[]{:S(2)}) %collective-permute-start.27) | collective-permute-done | bytes 1572896 | tf_op jit(solution)/shard_map/ppermute | solution.py:23
  108.9 18.6 %collective-permute-done.25.rest_3_ = bf16[2,1536,256]{2,1,0:T(8,128)(2,1)S(1)} collective-permute-done((bf16[2,1536,256]{2,1,0:T(8,128)(2,1)}, bf16[2,1536,256]{2,1,0:T(8,128)(2,1)S(1)}, u32[]{:S(2)}, u32[]{:S(2)}) %collective-permute-start.25) | collective-permute-done | bytes 1572896 | tf_op jit(solution)/shard_map/ppermute | solution.py:32
  135.8 13.1 %shard_map.60 = (f32[512,8192]{1,0:T(8,128)}, f32[8,128]{1,0:T(8,128)}, bf16[512,1536]{1,0:T(8,128)(2,1)}) custom-call(s32[8]{0:T(128)} %stack.164.ids_ref, f32[1]{0:T(128)} %bitcast.2.scale_ref, bf16[2,1536,256]{2,1,0:T(8,128)(2,1)} %get-tuple-element.71.rest_0_.rest_1_, bf16[2,1536,256]{2,1,0:T(8,128)(2,1)} %get-tuple-element.71.rest_0_.rest_1_, ...), custom_call_target="tpu_custom_call" | custom-call | flops 1150000000 | bytes 1000000 | tf_op jit(solution)/shard_map/pallas_call | solution.py:265
  149.0 16.9 %collective-permute-done.33.rest_1_ = bf16[2,1536,256]{2,1,0:T(8,128)(2,1)S(1)} collective-permute-done((bf16[2,1536,256]{2,1,0:T(8,128)(2,1)}, bf16[2,1536,256]{2,1,0:T(8,128)(2,1)S(1)}, u32[]{:S(2)}, u32[]{:S(2)}) %collective-permute-start.33) | collective-permute-done | bytes 1572896 | tf_op jit(solution)/shard_map/ppermute | solution.py:32
  169.3 1.7 collective-permute-start.32
  171.6 2.3 %collective-permute-done.38.rest_6_ = bf16[2,1536,256]{2,1,0:T(8,128)(2,1)} collective-permute-done((bf16[2,1536,256]{2,1,0:T(8,128)(2,1)S(1)}, bf16[2,1536,256]{2,1,0:T(8,128)(2,1)}, u32[]{:S(2)}, u32[]{:S(2)}) %collective-permute-start.38) | collective-permute-done | bytes 1572896 | tf_op jit(solution)/shard_map/ppermute | solution.py:32
  174.1 10.1 %shard_map.61 = (f32[512,8192]{1,0:T(8,128)}, f32[8,128]{1,0:T(8,128)}) custom-call(s32[6]{0:T(128)} %stack.203.ids_ref, f32[1]{0:T(128)} %bitcast.2.scale_ref, bf16[512,1536]{1,0:T(8,128)(2,1)} %get-tuple-element.78.rest_0_, bf16[2,1536,256]{2,1,0:T(8,128)(2,1)} %copy-done, ...), custom_call_target="tpu_custom_call", output_to_operand_aliasing={{0}: (10, {})} | custom-call | flops 1150000000 | bytes 1000000 | tf_op jit(solution)/shard_map/pallas_call | solution.py:265
  185.5 2.5 %collective-permute-done.39.rest_3_ = bf16[2,512,256]{2,1,0:T(8,128)(2,1)S(1)} collective-permute-done((bf16[2,512,256]{2,1,0:T(8,128)(2,1)}, bf16[2,512,256]{2,1,0:T(8,128)(2,1)S(1)}, u32[]{:S(2)}, u32[]{:S(2)}) %collective-permute-start.39) | collective-permute-done | bytes 524320 | tf_op jit(solution)/shard_map/ppermute | solution.py:32
  189.2 6.3 %shard_map.62 = (f32[512,8192]{1,0:T(8,128)}, f32[8,128]{1,0:T(8,128)}) custom-call(s32[2]{0:T(128)} %pad_add_fusion.ids_ref, f32[1]{0:T(128)} %bitcast.2.scale_ref, bf16[512,1536]{1,0:T(8,128)(2,1)} %get-tuple-element.78.rest_0_, bf16[2,512,256]{2,1,0:T(8,128)(2,1)} %collective-permute-done.32.rest_1_, ...), custom_call_target="tpu_custom_call", output_to_operand_aliasing={{0}: (8, {})} | custom-call | flops 1150000000 | bytes 1000000 | tf_op jit(solution)/shard_map/pallas_call | solution.py:265
  (140 shorter events, 40.7 us)
Async XLA Ops:
  11.8 8.2 %collective-permute-start.4 = (bf16[2,16,3200]{2,1,0:T(8,128)(2,1)S(1)}, bf16[2,16,3200]{2,1,0:T(8,128)(2,1)S(1)}, u32[]{:S(2)}, u32[]{:S(2)}) collective-permute-start(bf16[2,16,3200]{2,1,0:T(8,128)(2,1)S(1)} %pad_maximum_fusion), channel_id=1, source_target_pairs={{0,96},{1,33},{32,0},{33,65},{64,32},{65,97},{96,64},{97,1},{2,98}... | collective-permute-start | bytes 614408 | tf_op jit(solution)/shard_map/ppermute | solution.py:28
  11.8 10.4 %collective-permute-start.6 = (bf16[2,16,3200]{2,1,0:T(8,128)(2,1)S(1)}, bf16[2,16,3200]{2,1,0:T(8,128)(2,1)S(1)}, u32[]{:S(2)}, u32[]{:S(2)}) collective-permute-start(bf16[2,16,3200]{2,1,0:T(8,128)(2,1)S(1)} %pad_maximum_fusion), channel_id=1, source_target_pairs={{0,64},{32,96},{64,0},{96,32},{1,65},{33,97},{65,1},{97,33},{2,66}... | collective-permute-start | bytes 614408 | tf_op jit(solution)/shard_map/ppermute | solution.py:355
  13.5 10.7 %collective-permute-start.1 = (bf16[2,16,3200]{2,1,0:T(8,128)(2,1)S(1)}, bf16[2,16,3200]{2,1,0:T(8,128)(2,1)S(1)}, u32[]{:S(2)}, u32[]{:S(2)}) collective-permute-start(bf16[2,16,3200]{2,1,0:T(8,128)(2,1)S(1)} %pad_maximum_fusion), channel_id=1, source_target_pairs={{0,1},{1,0},{2,3},{3,2},{4,5},{5,4},{6,7},{7,6},{8,9},{9,8},{10,11... | collective-permute-start | bytes 614408 | tf_op jit(solution)/shard_map/ppermute | solution.py:32
  15.5 8.6 %collective-permute-start.3 = (bf16[2,16,3200]{2,1,0:T(8,128)(2,1)S(1)}, bf16[2,16,3200]{2,1,0:T(8,128)(2,1)S(1)}, u32[]{:S(2)}, u32[]{:S(2)}) collective-permute-start(bf16[2,16,3200]{2,1,0:T(8,128)(2,1)S(1)} %collective-permute-done.2), channel_id=1, source_target_pairs={{0,1},{1,0},{2,3},{3,2},{4,5},{5,4},{6,7},{7,6},{8,9},{9,8},{10,11... | collective-permute-start | bytes 614408 | tf_op jit(solution)/shard_map/ppermute | solution.py:32
  29.6 10.5 %collective-permute-start.8 = (bf16[2,96,1536]{2,1,0:T(8,128)(2,1)}, bf16[2,96,1536]{2,1,0:T(8,128)(2,1)S(1)}, u32[]{:S(2)}, u32[]{:S(2)}) collective-permute-start(bf16[2,96,1536]{2,1,0:T(8,128)(2,1)} %get-tuple-element.49.rest_0_), channel_id=1, source_target_pairs={{0,4},{1,13},{4,8},{5,1},{8,12},{9,5},{12,0},{13,9},{2,6},{3,15},{... | collective-permute-start | bytes 1769480 | tf_op jit(solution)/shard_map/ppermute | solution.py:23
  32.2 15.2 %collective-permute-start.10 = (bf16[2,96,1536]{2,1,0:T(8,128)(2,1)}, bf16[2,96,1536]{2,1,0:T(8,128)(2,1)S(1)}, u32[]{:S(2)}, u32[]{:S(2)}) collective-permute-start(bf16[2,96,1536]{2,1,0:T(8,128)(2,1)} %get-tuple-element.49.rest_0_), channel_id=1, source_target_pairs={{0,2},{2,0},{1,3},{3,1},{4,6},{6,4},{5,7},{7,5},{8,10},{10,8},{9,1... | collective-permute-start | bytes 1769480 | tf_op jit(solution)/shard_map/ppermute | solution.py:32
  32.2 15.2 %collective-permute-start.11 = (bf16[2,96,1536]{2,1,0:T(8,128)(2,1)}, bf16[2,96,1536]{2,1,0:T(8,128)(2,1)S(1)}, u32[]{:S(2)}, u32[]{:S(2)}) collective-permute-start(bf16[2,96,1536]{2,1,0:T(8,128)(2,1)} %get-tuple-element.50.rest_1_), channel_id=1, source_target_pairs={{0,4},{1,13},{4,8},{5,1},{8,12},{9,5},{12,0},{13,9},{2,6},{3,15},{... | collective-permute-start | bytes 1769480 | tf_op jit(solution)/shard_map/ppermute | solution.py:23
  48.4 12.1 %collective-permute-start.9 = (bf16[2,96,1536]{2,1,0:T(8,128)(2,1)S(1)}, bf16[2,96,1536]{2,1,0:T(8,128)(2,1)S(1)}, u32[]{:S(2)}, u32[]{:S(2)}) collective-permute-start(bf16[2,96,1536]{2,1,0:T(8,128)(2,1)S(1)} %collective-permute-done.8.rest_2_), channel_id=1, source_target_pairs={{0,4},{1,13},{4,8},{5,1},{8,12},{9,5},{12,0},{13,9},{2,6},{3,15},{... | collective-permute-start | bytes 1769480 | tf_op jit(solution)/shard_map/ppermute | solution.py:23
  49.5 14.9 %collective-permute-start.16 = (bf16[2,96,1536]{2,1,0:T(8,128)(2,1)S(1)}, bf16[2,96,1536]{2,1,0:T(8,128)(2,1)S(1)}, u32[]{:S(2)}, u32[]{:S(2)}) collective-permute-start(bf16[2,96,1536]{2,1,0:T(8,128)(2,1)S(1)} %collective-permute-done.8.rest_2_), channel_id=1, source_target_pairs={{0,2},{2,0},{1,3},{3,1},{4,6},{6,4},{5,7},{7,5},{8,10},{10,8},{9,1... | collective-permute-start | bytes 1769480 | tf_op jit(solution)/shard_map/ppermute | solution.py:32
  49.6 15.2 %collective-permute-start.18 = (bf16[2,96,1536]{2,1,0:T(8,128)(2,1)}, bf16[2,96,1536]{2,1,0:T(8,128)(2,1)S(1)}, u32[]{:S(2)}, u32[]{:S(2)}) collective-permute-start(bf16[2,96,1536]{2,1,0:T(8,128)(2,1)} %collective-permute-done.12.rest_1_), channel_id=1, source_target_pairs={{0,4},{1,13},{4,8},{5,1},{8,12},{9,5},{12,0},{13,9},{2,6},{3,15},{... | collective-permute-start | bytes 1769480 | tf_op jit(solution)/shard_map/ppermute | solution.py:23
  66.7 12.0 %collective-permute-start.17 = (bf16[2,64,1536]{2,1,0:T(8,128)(2,1)}, bf16[2,64,1536]{2,1,0:T(8,128)(2,1)}, u32[]{:S(2)}, u32[]{:S(2)}) collective-permute-start(bf16[2,64,1536]{2,1,0:T(8,128)(2,1)} %slice.13), channel_id=1, source_target_pairs={{0,4},{1,13},{4,8},{5,1},{8,12},{9,5},{12,0},{13,9},{2,6},{3,15},{... | collective-permute-start | bytes 1179656 | tf_op jit(solution)/shard_map/ppermute | solution.py:23
  67.7 11.0 %collective-permute-start.15 = (bf16[2,32,1536]{2,1,0:T(8,128)(2,1)}, bf16[2,32,1536]{2,1,0:T(8,128)(2,1)}, u32[]{:S(2)}, u32[]{:S(2)}) collective-permute-start(bf16[2,32,1536]{2,1,0:T(8,128)(2,1)} %slice.12), channel_id=1, source_target_pairs={{0,2},{2,0},{1,3},{3,1},{4,6},{6,4},{5,7},{7,5},{8,10},{10,8},{9,1... | collective-permute-start | bytes 589832 | tf_op jit(solution)/shard_map/ppermute | solution.py:32
  89.0 19.9 %collective-permute-start.27 = (bf16[2,1536,256]{2,1,0:T(8,128)(2,1)}, bf16[2,1536,256]{2,1,0:T(8,128)(2,1)}, u32[]{:S(2)}, u32[]{:S(2)}) collective-permute-start(bf16[2,1536,256]{2,1,0:T(8,128)(2,1)} %get-tuple-element.71.rest_0_.rest_1_), channel_id=1, source_target_pairs={{0,4},{1,13},{4,8},{5,1},{8,12},{9,5},{12,0},{13,9},{2,6},{3,15},{... | collective-permute-start | bytes 4718600 | tf_op jit(solution)/shard_map/ppermute | solution.py:23
  91.1 36.4 %collective-permute-start.25 = (bf16[2,1536,256]{2,1,0:T(8,128)(2,1)}, bf16[2,1536,256]{2,1,0:T(8,128)(2,1)S(1)}, u32[]{:S(2)}, u32[]{:S(2)}) collective-permute-start(bf16[2,1536,256]{2,1,0:T(8,128)(2,1)} %get-tuple-element.71.rest_0_.rest_1_), channel_id=1, source_target_pairs={{0,2},{2,0},{1,3},{3,1},{4,6},{6,4},{5,7},{7,5},{8,10},{10,8},{9,1... | collective-permute-start | bytes 4718600 | tf_op jit(solution)/shard_map/ppermute | solution.py:32
  92.8 34.7 %collective-permute-start.26 = (bf16[2,1536,256]{2,1,0:T(8,128)(2,1)S(1)}, bf16[2,1536,256]{2,1,0:T(8,128)(2,1)}, u32[]{:S(2)}, u32[]{:S(2)}) collective-permute-start(bf16[2,1536,256]{2,1,0:T(8,128)(2,1)S(1)} %collective-permute-done.24.rest_2_), channel_id=1, source_target_pairs={{0,4},{1,13},{4,8},{5,1},{8,12},{9,5},{12,0},{13,9},{2,6},{3,15},{... | collective-permute-start | bytes 4718600 | tf_op jit(solution)/shard_map/ppermute | solution.py:23
  128.0 7.9 %collective-permute-start.30 = (bf16[2,1536,256]{2,1,0:T(8,128)(2,1)}, bf16[2,1536,256]{2,1,0:T(8,128)(2,1)}, u32[]{:S(2)}, u32[]{:S(2)}) collective-permute-start(bf16[2,1536,256]{2,1,0:T(8,128)(2,1)} %collective-permute-done.27.rest_5_), channel_id=1, source_target_pairs={{0,1},{1,0},{2,3},{3,2},{4,5},{5,4},{6,7},{7,6},{8,9},{9,8},{10,11... | collective-permute-start | bytes 4718600 | tf_op jit(solution)/shard_map/ppermute | solution.py:32
  128.1 7.8 %collective-permute-start.29 = (bf16[2,1536,256]{2,1,0:T(8,128)(2,1)}, bf16[2,1536,256]{2,1,0:T(8,128)(2,1)}, u32[]{:S(2)}, u32[]{:S(2)}) collective-permute-start(bf16[2,1536,256]{2,1,0:T(8,128)(2,1)} %collective-permute-done.26.rest_6_), channel_id=1, source_target_pairs={{0,1},{1,0},{2,3},{3,2},{4,5},{5,4},{6,7},{7,6},{8,9},{9,8},{10,11... | collective-permute-start | bytes 4718600 | tf_op jit(solution)/shard_map/ppermute | solution.py:32
  128.5 20.5 %collective-permute-start.31 = (bf16[2,1536,256]{2,1,0:T(8,128)(2,1)}, bf16[2,1536,256]{2,1,0:T(8,128)(2,1)S(1)}, u32[]{:S(2)}, u32[]{:S(2)}) collective-permute-start(bf16[2,1536,256]{2,1,0:T(8,128)(2,1)} %collective-permute-done.27.rest_5_), channel_id=1, source_target_pairs={{0,4},{1,13},{4,8},{5,1},{8,12},{9,5},{12,0},{13,9},{2,6},{3,15},{... | collective-permute-start | bytes 4718600 | tf_op jit(solution)/shard_map/ppermute | solution.py:23
  129.4 36.5 %collective-permute-start.33 = (bf16[2,1536,256]{2,1,0:T(8,128)(2,1)}, bf16[2,1536,256]{2,1,0:T(8,128)(2,1)S(1)}, u32[]{:S(2)}, u32[]{:S(2)}) collective-permute-start(bf16[2,1536,256]{2,1,0:T(8,128)(2,1)} %collective-permute-done.27.rest_5_), channel_id=1, source_target_pairs={{0,2},{2,0},{1,3},{3,1},{4,6},{6,4},{5,7},{7,5},{8,10},{10,8},{9,1... | collective-permute-start | bytes 4718600 | tf_op jit(solution)/shard_map/ppermute | solution.py:32
  132.3 34.0 %collective-permute-start.35 = (bf16[2,1536,256]{2,1,0:T(8,128)(2,1)}, bf16[2,1536,256]{2,1,0:T(8,128)(2,1)}, u32[]{:S(2)}, u32[]{:S(2)}) collective-permute-start(bf16[2,1536,256]{2,1,0:T(8,128)(2,1)} %collective-permute-done.28.rest_4_), channel_id=1, source_target_pairs={{0,4},{1,13},{4,8},{5,1},{8,12},{9,5},{12,0},{13,9},{2,6},{3,15},{... | collective-permute-start | bytes 4718600 | tf_op jit(solution)/shard_map/ppermute | solution.py:23
  165.9 8.0 %collective-permute-start.38 = (bf16[2,1536,256]{2,1,0:T(8,128)(2,1)S(1)}, bf16[2,1536,256]{2,1,0:T(8,128)(2,1)}, u32[]{:S(2)}, u32[]{:S(2)}) collective-permute-start(bf16[2,1536,256]{2,1,0:T(8,128)(2,1)S(1)} %collective-permute-done.31.rest_5_), channel_id=1, source_target_pairs={{0,1},{1,0},{2,3},{3,2},{4,5},{5,4},{6,7},{7,6},{8,9},{9,8},{10,11... | collective-permute-start | bytes 4718600 | tf_op jit(solution)/shard_map/ppermute | solution.py:32
  166.4 7.7 %collective-permute-start.36 = (bf16[2,1536,256]{2,1,0:T(8,128)(2,1)}, bf16[2,1536,256]{2,1,0:T(8,128)(2,1)}, u32[]{:S(2)}, u32[]{:S(2)}) collective-permute-start(bf16[2,1536,256]{2,1,0:T(8,128)(2,1)} %collective-permute-done.35.rest_2_), channel_id=1, source_target_pairs={{0,1},{1,0},{2,3},{3,2},{4,5},{5,4},{6,7},{7,6},{8,9},{9,8},{10,11... | collective-permute-start | bytes 4718600 | tf_op jit(solution)/shard_map/ppermute | solution.py:32
  168.4 15.8 %collective-permute-start.34 = (bf16[2,1024,256]{2,1,0:T(8,128)(2,1)}, bf16[2,1024,256]{2,1,0:T(8,128)(2,1)}, u32[]{:S(2)}, u32[]{:S(2)}) collective-permute-start(bf16[2,1024,256]{2,1,0:T(8,128)(2,1)} %slice.15), channel_id=1, source_target_pairs={{0,4},{1,13},{4,8},{5,1},{8,12},{9,5},{12,0},{13,9},{2,6},{3,15},{... | collective-permute-start | bytes 3145736 | tf_op jit(solution)/shard_map/ppermute | solution.py:23
  169.3 15.0 %collective-permute-start.32 = (bf16[2,512,256]{2,1,0:T(8,128)(2,1)}, bf16[2,512,256]{2,1,0:T(8,128)(2,1)}, u32[]{:S(2)}, u32[]{:S(2)}) collective-permute-start(bf16[2,512,256]{2,1,0:T(8,128)(2,1)} %slice.14), channel_id=1, source_target_pairs={{0,2},{2,0},{1,3},{3,1},{4,6},{6,4},{5,7},{7,5},{8,10},{10,8},{9,1... | collective-permute-start | bytes 1572872 | tf_op jit(solution)/shard_map/ppermute | solution.py:32
  (43 other events, 262.3 us)

commit v2 on v1

--- a/solution.py
+++ b/solution.py
@@ -102,7 +102,7 @@
     )(expert, base, *blocks)
 
 
-def ffn_kernel(blocks, n_arrays, n_old, offsets_ref, *rest):
+def ffn_kernel(blocks, first, n_arrays, n_old, offsets_ref, *rest):
     arrays, (gate_hbm, up_hbm) = rest[:n_arrays], rest[n_arrays : n_arrays + 2]
     (
         out_ref,
@@ -154,7 +154,7 @@
         up = jnp.dot(rows[...], up_held[:, cols], preferred_element_type=jnp.float32)
         result[q] = (gate / (1.0 + jnp.exp(-gate)) * up).astype(jnp.bfloat16)
         for i in range(len(blocks)):
-            to = pl.ds(pl.multiple_of(offsets_ref[i], 16), piece_rows)
+            to = pl.ds(pl.multiple_of(offsets_ref[first + i], 16), piece_rows)
             sent.append(
                 pltpu.make_async_copy(
                     result.at[q, pl.ds(i * piece_rows, piece_rows)],
@@ -182,14 +182,14 @@
     return arrays, sources, start
 
 
-def ffn(offsets, blocks, wg, wu, total_rows, token, old=()):
+def ffn(offsets, first, blocks, wg, wu, total_rows, token, old=()):
     arrays, sources, piece_rows = indexed(blocks)
     width, panel = wg.shape
     rows = len(blocks) * piece_rows
     out = jax.ShapeDtypeStruct((2, total_rows, panel // 2), jnp.bfloat16)
     first_old = 4 + len(arrays)
     return pl.pallas_call(
-        functools.partial(ffn_kernel, sources, len(arrays), len(old) + 1),
+        functools.partial(ffn_kernel, sources, first, len(arrays), len(old) + 1),
         out_shape=(out, jax.ShapeDtypeStruct((8, 128), jnp.float32)),
         in_specs=[SMEM] + [ANY] * (len(arrays) + 3 + len(old)),
         out_specs=(ANY, VMEM),
@@ -209,7 +209,7 @@
     )(offsets, *arrays, wg, wu, token, *old)
 
 
-def gram_kernel(sources, n_arrays, first, extra, ids_ref, scale_ref, *rest):
+def gram_kernel(sources, start, n_arrays, first, extra, ids_ref, scale_ref, *rest):
     own_ref, *arrays = rest[: 1 + n_arrays]
     out_ref, token_ref, *rest = rest[1 + n_arrays + extra :]
     if first:
@@ -222,8 +222,8 @@
 
     def fetch(p):
         copies = []
-        for k, (array, start, rows) in enumerate(sources[p]):
-            target = held.at[p % depth, :, pl.ds(start, rows)]
+        for k, (array, row, rows) in enumerate(sources[p]):
+            target = held.at[p % depth, :, pl.ds(row, rows)]
             copies.append(pltpu.make_async_copy(arrays[array], target, in_sems.at[p % depth, k]))
             copies[-1].start()
         return copies
@@ -249,21 +249,21 @@
             result[p % 2, :, side * half : (side + 1) * half] = total * scale_ref[0]
         if p + depth < count:
             fetched[p + depth] = fetch(p + depth)
-        cols = pl.ds(pl.multiple_of(ids_ref[p] * 2 * half, 2 * half), 2 * half)
+        cols = pl.ds(pl.multiple_of(ids_ref[start + p] * 2 * half, 2 * half), 2 * half)
         sent[p] = pltpu.make_async_copy(result.at[p % 2], out_ref.at[:, cols], out_sems.at[p % 2])
         sent[p].start()
     for p in range(max(0, count - 2), count):
         sent[p].wait()
 
 
-def gram(ids, scale, own, pairs, features, token, old=None):
+def gram(ids, start, scale, own, pairs, features, token, old=None):
     arrays, sources, rows = indexed(pairs)
     half = arrays[0].shape[2]
     first = own.ndim == 3
     extra = 1 if old is None else 2
     turned = ((2 * half, rows), jnp.bfloat16)
     return pl.pallas_call(
-        functools.partial(gram_kernel, sources, len(arrays), first, extra),
+        functools.partial(gram_kernel, sources, start, len(arrays), first, extra),
         out_shape=(
             jax.ShapeDtypeStruct((2 * half, features), jnp.float32),
             jax.ShapeDtypeStruct((8, 128), jnp.float32),
@@ -371,11 +371,13 @@
     def chip(at, dl):
         return (place_of[at] % 4) * 2 + (l + dl) % 2
 
-    def offsets(chips):
-        rows = [
-            (chip(at, dl) * 2 + (c + half) % 2) * block for at, dl in chips for half in (0, 1)
-        ]
-        return jnp.stack(rows).astype(jnp.int32)
+    chips_all = [("o", 0), ("o", 1), ("m", 0), ("p", 0), ("m", 1), ("p", 1), ("f", 0), ("f", 1)]
+    ids = [chip(at, dl) * 2 + (c + core) % 2 for at, dl in chips_all for core in (0, 1)]
+    ids = jnp.stack(ids).astype(jnp.int32)
+    offsets = ids * block
+
+    def place_in(chips):
+        return 2 * chips_all.index(chips[0])
 
     def blocks_of(spread, chips):
         return [spread.found[at, dl, core] for at, dl in chips for core in (0, 1)]
@@ -383,9 +385,8 @@
     total = 16 * block
 
     def hidden_of(chips, token, *old):
-        return ffn(
-            offsets(chips), blocks_of(rows, chips), gate_panel, up_panel, total, token, old
-        )
+        found = blocks_of(rows, chips)
+        return ffn(offsets, place_in(chips), found, gate_panel, up_panel, total, token, old)
 
     token = jnp.zeros((8, 128), jnp.float32)
     rows = Spread()
@@ -399,9 +400,8 @@
     hidden, token = hidden_of([("f", 1)], token, hidden)
 
     def part(chips, token, old=None):
-        ids = [chip(at, dl) * 2 + (c + core) % 2 for at, dl in chips for core in (0, 1)]
-        ids = jnp.stack(ids).astype(jnp.int32)
-        return gram(ids, scale, own, blocks_of(panels, chips), features, token, old)
+        found = blocks_of(panels, chips)
+        return gram(ids, place_in(chips), scale, own, found, features, token, old)
 
     panels = Spread()
     panels.open(hidden)

time: 196 us -> 196 us (level)
  waiting for transfers between devices: 74.2 us -> 80.2 us
  starting transfers between devices: 41 us -> 38.1 us
    ppermute x27, waiting for transfers between devices: 54.9 us -> 60.4 us  [swap(): return lax.ppermute(a, axis, [(0, 1), (1, 0)])]
    ppermute x11, starting transfers between devices: 14.5 us -> 11.5 us  [ring_hop(): return lax.ppermute(a, (axis, 'c'), pairs)]
    another operation x4 -> x1, local copies, waits for them, and re-layouts: 2.47 us -> 0.09 us  [local(): ids = jnp.stack(ids).astype(jnp.int32)]
    unnamed x53 -> x71, local copies, waits for them, and re-layouts: 3.35 us -> 5.29 us
  transfers between devices with their start and end apart: 41 -> 41, of which waited for: 15 -> 19; matrix products, arithmetic and copies ran while one was open for 5% -> 2% of each run, Pallas kernels for 24% -> 24%
where the time goes in v2:
time: 196 us
  waiting for transfers between devices  80.2 us (41%)
  Pallas kernels  64.4 us (33%)
  starting transfers between devices  38.1 us (19%)
  local copies, waits for them, and re-layouts  8.77 us (4%)
  other arithmetic  2.77 us (1%)
    ppermute x27, waiting for transfers between devices, swap(): return lax.ppermute(a, axis, [(0, 1), (1, 0)])  60.4 us
    pallas_call x4, Pallas kernels, ffn(): pl.pallas_call(functools.partial(ffn_kernel, sources, first, len(arrays),...  31 us
    pallas_call x3, Pallas kernels, gram(): pl.pallas_call(functools.partial(gram_kernel, sources, start, len(arrays)...  29.4 us
    ppermute x27, starting transfers between devices, swap(): return lax.ppermute(a, axis, [(0, 1), (1, 0)])  20.3 us
    ppermute x11, waiting for transfers between devices, ring_hop(): return lax.ppermute(a, (axis, 'c'), pairs)  15.1 us
    ppermute x11, starting transfers between devices, ring_hop(): return lax.ppermute(a, (axis, 'c'), pairs)  11.5 us
    unnamed x71, local copies, waits for them, and re-layouts  5.29 us
    ppermute x1, starting transfers between devices, far_swap(): return lax.ppermute(a, ('h', 'l'), [(0, 3), (3, 0), (1, 2), (2, 1)])  4.67 us
  transfers between devices with their start and end apart: 41, of which 19 were waited for; matrix products, arithmetic and copies ran while one was open for 2% of the time, Pallas kernels for 24%

profile of v2, /device:TPU:1, one launch (start us, length us, event | category | flops | bytes accessed | tf_op | source)
XLA Modules:
  0.0 195.6 jit_solution(10493396735408447835)
XLA Ops:
  1.7 4.7 %collective-permute-start = (bf16[16,3200]{1,0:T(8,128)(2,1)S(1)}, bf16[16,3200]{1,0:T(8,128)(2,1)S(1)}, u32[]{:S(2)}, u32[]{:S(2)}) collective-permute-start(bf16[16,3200]{1,0:T(8,128)(2,1)S(1)} %get-tuple-element.94), channel_id=1, source_target_pairs={{0,18},{18,0},{2,16},{16,2},{1,19},{19,1},{3,17},{17,3},{4,22},{22... | collective-permute-start | bytes 307208 | tf_op jit(solution)/shard_map/ppermute | solution.py:36
  6.4 2.6 %collective-permute-done = bf16[16,3200]{1,0:T(8,128)(2,1)S(1)} collective-permute-done((bf16[16,3200]{1,0:T(8,128)(2,1)S(1)}, bf16[16,3200]{1,0:T(8,128)(2,1)S(1)}, u32[]{:S(2)}, u32[]{:S(2)}) %collective-permute-start) | collective-permute-done | bytes 102432 | tf_op jit(solution)/shard_map/ppermute | solution.py:36
  9.0 2.8 %collective-permute-start.2 = (bf16[2,16,3200]{2,1,0:T(8,128)(2,1)S(1)}, bf16[2,16,3200]{2,1,0:T(8,128)(2,1)S(1)}, u32[]{:S(2)}, u32[]{:S(2)}) collective-permute-start(bf16[2,16,3200]{2,1,0:T(8,128)(2,1)S(1)} %pad_maximum_fusion), channel_id=1, source_target_pairs={{0,32},{1,97},{32,64},{33,1},{64,96},{65,33},{96,0},{97,65},{2,34}... | collective-permute-start | bytes 614408 | tf_op jit(solution)/shard_map/ppermute | solution.py:23
  13.5 2.1 %collective-permute-start.1 = (bf16[2,16,3200]{2,1,0:T(8,128)(2,1)S(1)}, bf16[2,16,3200]{2,1,0:T(8,128)(2,1)S(1)}, u32[]{:S(2)}, u32[]{:S(2)}) collective-permute-start(bf16[2,16,3200]{2,1,0:T(8,128)(2,1)S(1)} %pad_maximum_fusion), channel_id=1, source_target_pairs={{0,1},{1,0},{2,3},{3,2},{4,5},{5,4},{6,7},{7,6},{8,9},{9,8},{10,11... | collective-permute-start | bytes 614408 | tf_op jit(solution)/shard_map/ppermute | solution.py:32
  15.5 3.1 %collective-permute-start.3 = (bf16[2,16,3200]{2,1,0:T(8,128)(2,1)S(1)}, bf16[2,16,3200]{2,1,0:T(8,128)(2,1)S(1)}, u32[]{:S(2)}, u32[]{:S(2)}) collective-permute-start(bf16[2,16,3200]{2,1,0:T(8,128)(2,1)S(1)} %collective-permute-done.2), channel_id=1, source_target_pairs={{0,1},{1,0},{2,3},{3,2},{4,5},{5,4},{6,7},{7,6},{8,9},{9,8},{10,11... | collective-permute-start | bytes 614408 | tf_op jit(solution)/shard_map/ppermute | solution.py:32
  25.6 4.0 %shard_map.55 = (bf16[2,96,1536]{2,1,0:T(8,128)(2,1)}, bf16[2,96,1536]{2,1,0:T(8,128)(2,1)}) custom-call(s32[1]{0:T(128)} %bitcast.17.expert_ref, f32[8,256]{1,0:T(8,128)} %broadcast_in_dim.18.base_ref, bf16[32,3200]{1,0:T(8,128)(2,1)} %bitcast.48, bf16[32,3200]{1,0:T(8,128)(2,1)} %bitcast.53, bf16[32,3200]{1,0:T(8,128)(2,1)} %bitcast.50, ...), custom_call_target="tpu_custom_call" | custom-call | flops 3449999872 | bytes 1000000 | tf_op jit(solution)/shard_map/pallas_call | solution.py:90
  29.6 2.5 %collective-permute-start.8 = (bf16[2,96,1536]{2,1,0:T(8,128)(2,1)}, bf16[2,96,1536]{2,1,0:T(8,128)(2,1)S(1)}, u32[]{:S(2)}, u32[]{:S(2)}) collective-permute-start(bf16[2,96,1536]{2,1,0:T(8,128)(2,1)} %get-tuple-element.49.rest_0_), channel_id=1, source_target_pairs={{0,4},{1,13},{4,8},{5,1},{8,12},{9,5},{12,0},{13,9},{2,6},{3,15},{... | collective-permute-start | bytes 1769480 | tf_op jit(solution)/shard_map/ppermute | solution.py:23
  33.9 6.2 %shard_map.56 = (bf16[2,1536,256]{2,1,0:T(8,128)(2,1)}, f32[8,128]{1,0:T(8,128)}) custom-call(s32[16]{0:T(128)} %broadcast_multiply_fusion.offsets_ref, bf16[2,96,1536]{2,1,0:T(8,128)(2,1)} %get-tuple-element.49.rest_0_, bf16[2,96,1536]{2,1,0:T(8,128)(2,1)} %get-tuple-element.50.rest_1_, bf16[3072,512]{1,0:T(8,128)(2,1)} %bitcast.40, ...), custom_call_target="tpu_custom_call" | custom-call | flops 1150000000 | bytes 1000000 | tf_op jit(solution)/shard_map/pallas_call | solution.py:191
  40.2 7.2 %collective-permute-done.10.rest_0_ = bf16[2,96,1536]{2,1,0:T(8,128)(2,1)S(1)} collective-permute-done((bf16[2,96,1536]{2,1,0:T(8,128)(2,1)}, bf16[2,96,1536]{2,1,0:T(8,128)(2,1)S(1)}, u32[]{:S(2)}, u32[]{:S(2)}) %collective-permute-start.10) | collective-permute-done | bytes 589856 | tf_op jit(solution)/shard_map/ppermute | solution.py:32
  52.0 9.1 %shard_map.57 = (bf16[2,1536,256]{2,1,0:T(8,128)(2,1)}, f32[8,128]{1,0:T(8,128)}) custom-call(s32[16]{0:T(128)} %broadcast_multiply_fusion.offsets_ref, bf16[2,96,1536]{2,1,0:T(8,128)(2,1)} %copy-done.11, bf16[2,96,1536]{2,1,0:T(8,128)(2,1)} %copy-done.14, bf16[2,96,1536]{2,1,0:T(8,128)(2,1)} %copy-done.10, ...), custom_call_target="tpu_custom_call", output_to_operand_aliasing={{0}: (10, {})} | custom-call | flops 1150000000 | bytes 1000000 | tf_op jit(solution)/shard_map/pallas_call | solution.py:191
  61.2 3.1 %collective-permute-done.16.rest_0_ = bf16[2,96,1536]{2,1,0:T(8,128)(2,1)S(1)} collective-permute-done((bf16[2,96,1536]{2,1,0:T(8,128)(2,1)S(1)}, bf16[2,96,1536]{2,1,0:T(8,128)(2,1)S(1)}, u32[]{:S(2)}, u32[]{:S(2)}) %collective-permute-start.16) | collective-permute-done | bytes 589856 | tf_op jit(solution)/shard_map/ppermute | solution.py:32
  68.8 9.1 %shard_map.58 = (bf16[2,1536,256]{2,1,0:T(8,128)(2,1)}, f32[8,128]{1,0:T(8,128)}) custom-call(s32[16]{0:T(128)} %broadcast_multiply_fusion.offsets_ref, bf16[2,96,1536]{2,1,0:T(8,128)(2,1)} %copy-done.2, bf16[2,96,1536]{2,1,0:T(8,128)(2,1)} %copy-done.13, bf16[2,96,1536]{2,1,0:T(8,128)(2,1)} %copy-done.19, ...), custom_call_target="tpu_custom_call", output_to_operand_aliasing={{0}: (10, {})} | custom-call | flops 1150000000 | bytes 1000000 | tf_op jit(solution)/shard_map/pallas_call | solution.py:191
  81.0 6.5 %shard_map.59 = (bf16[2,1536,256]{2,1,0:T(8,128)(2,1)}, f32[8,128]{1,0:T(8,128)}) custom-call(s32[16]{0:T(128)} %broadcast_multiply_fusion.offsets_ref, bf16[2,32,1536]{2,1,0:T(8,128)(2,1)} %copy-done.24, bf16[2,64,1536]{2,1,0:T(8,128)(2,1)} %copy-done.21, bf16[2,32,1536]{2,1,0:T(8,128)(2,1)} %copy-done.25, ...), custom_call_target="tpu_custom_call", output_to_operand_aliasing={{0}: (8, {})} | custom-call | flops 1150000000 | bytes 1000000 | tf_op jit(solution)/shard_map/pallas_call | solution.py:191
  89.3 1.7 collective-permute-start.25
  92.5 15.1 %collective-permute-done.27.rest_5_ = bf16[2,1536,256]{2,1,0:T(8,128)(2,1)} collective-permute-done((bf16[2,1536,256]{2,1,0:T(8,128)(2,1)}, bf16[2,1536,256]{2,1,0:T(8,128)(2,1)}, u32[]{:S(2)}, u32[]{:S(2)}) %collective-permute-start.27) | collective-permute-done | bytes 1572896 | tf_op jit(solution)/shard_map/ppermute | solution.py:23
  107.6 18.5 %collective-permute-done.25.rest_3_ = bf16[2,1536,256]{2,1,0:T(8,128)(2,1)S(1)} collective-permute-done((bf16[2,1536,256]{2,1,0:T(8,128)(2,1)}, bf16[2,1536,256]{2,1,0:T(8,128)(2,1)S(1)}, u32[]{:S(2)}, u32[]{:S(2)}) %collective-permute-start.25) | collective-permute-done | bytes 1572896 | tf_op jit(solution)/shard_map/ppermute | solution.py:32
  127.5 1.7 collective-permute-start.33
  129.2 3.0 %collective-permute-done.28.rest_4_ = bf16[2,1536,256]{2,1,0:T(8,128)(2,1)} collective-permute-done((bf16[2,1536,256]{2,1,0:T(8,128)(2,1)S(1)}, bf16[2,1536,256]{2,1,0:T(8,128)(2,1)}, u32[]{:S(2)}, u32[]{:S(2)}) %collective-permute-start.28) | collective-permute-done | bytes 1572896 | tf_op jit(solution)/shard_map/ppermute | solution.py:32
  134.7 13.0 %shard_map.60 = (f32[512,8192]{1,0:T(8,128)}, f32[8,128]{1,0:T(8,128)}, bf16[512,1536]{1,0:T(8,128)(2,1)}) custom-call(s32[16]{0:T(128)} %copy-done.26, f32[1]{0:T(128)} %bitcast.16.scale_ref, bf16[2,1536,256]{2,1,0:T(8,128)(2,1)} %get-tuple-element.71.rest_0_.rest_1_, bf16[2,1536,256]{2,1,0:T(8,128)(2,1)} %get-tuple-element.71.rest_0_.rest_1_, ...), custom_call_target="tpu_custom_call" | custom-call | flops 1150000000 | bytes 1000000 | tf_op jit(solution)/shard_map/pallas_call | solution.py:265
  147.8 16.4 %collective-permute-done.33.rest_1_ = bf16[2,1536,256]{2,1,0:T(8,128)(2,1)S(1)} collective-permute-done((bf16[2,1536,256]{2,1,0:T(8,128)(2,1)}, bf16[2,1536,256]{2,1,0:T(8,128)(2,1)S(1)}, u32[]{:S(2)}, u32[]{:S(2)}) %collective-permute-start.33) | collective-permute-done | bytes 1572896 | tf_op jit(solution)/shard_map/ppermute | solution.py:32
  169.1 3.2 %collective-permute-done.38.rest_6_ = bf16[2,1536,256]{2,1,0:T(8,128)(2,1)S(1)} collective-permute-done((bf16[2,1536,256]{2,1,0:T(8,128)(2,1)S(1)}, bf16[2,1536,256]{2,1,0:T(8,128)(2,1)S(1)}, u32[]{:S(2)}, u32[]{:S(2)}) %collective-permute-start.38) | collective-permute-done | bytes 1572896 | tf_op jit(solution)/shard_map/ppermute | solution.py:32
  174.0 10.1 %shard_map.61 = (f32[512,8192]{1,0:T(8,128)}, f32[8,128]{1,0:T(8,128)}) custom-call(s32[16]{0:T(128)} %copy-done.26, f32[1]{0:T(128)} %bitcast.16.scale_ref, bf16[512,1536]{1,0:T(8,128)(2,1)} %get-tuple-element.78.rest_0_, bf16[2,1536,256]{2,1,0:T(8,128)(2,1)} %copy-done, ...), custom_call_target="tpu_custom_call", output_to_operand_aliasing={{0}: (10, {})} | custom-call | flops 1150000000 | bytes 1000000 | tf_op jit(solution)/shard_map/pallas_call | solution.py:265
  184.8 3.1 %collective-permute-done.39.rest_3_ = bf16[2,512,256]{2,1,0:T(8,128)(2,1)S(1)} collective-permute-done((bf16[2,512,256]{2,1,0:T(8,128)(2,1)}, bf16[2,512,256]{2,1,0:T(8,128)(2,1)S(1)}, u32[]{:S(2)}, u32[]{:S(2)}) %collective-permute-start.39) | collective-permute-done | bytes 524320 | tf_op jit(solution)/shard_map/ppermute | solution.py:32
  189.1 6.3 %shard_map.62 = (f32[512,8192]{1,0:T(8,128)}, f32[8,128]{1,0:T(8,128)}) custom-call(s32[16]{0:T(128)} %copy-done.26, f32[1]{0:T(128)} %bitcast.16.scale_ref, bf16[512,1536]{1,0:T(8,128)(2,1)} %get-tuple-element.78.rest_0_, bf16[2,512,256]{2,1,0:T(8,128)(2,1)} %collective-permute-done.32.rest_1_, ...), custom_call_target="tpu_custom_call", output_to_operand_aliasing={{0}: (8, {})} | custom-call | flops 1150000000 | bytes 1000000 | tf_op jit(solution)/shard_map/pallas_call | solution.py:265
  (153 shorter events, 39.0 us)
Async XLA Ops:
  1.7 7.3 %collective-permute-start = (bf16[16,3200]{1,0:T(8,128)(2,1)S(1)}, bf16[16,3200]{1,0:T(8,128)(2,1)S(1)}, u32[]{:S(2)}, u32[]{:S(2)}) collective-permute-start(bf16[16,3200]{1,0:T(8,128)(2,1)S(1)} %get-tuple-element.94), channel_id=1, source_target_pairs={{0,18},{18,0},{2,16},{16,2},{1,19},{19,1},{3,17},{17,3},{4,22},{22... | collective-permute-start | bytes 307208 | tf_op jit(solution)/shard_map/ppermute | solution.py:36
  11.8 8.2 %collective-permute-start.4 = (bf16[2,16,3200]{2,1,0:T(8,128)(2,1)S(1)}, bf16[2,16,3200]{2,1,0:T(8,128)(2,1)S(1)}, u32[]{:S(2)}, u32[]{:S(2)}) collective-permute-start(bf16[2,16,3200]{2,1,0:T(8,128)(2,1)S(1)} %pad_maximum_fusion), channel_id=1, source_target_pairs={{0,96},{1,33},{32,0},{33,65},{64,32},{65,97},{96,64},{97,1},{2,98}... | collective-permute-start | bytes 614408 | tf_op jit(solution)/shard_map/ppermute | solution.py:28
  11.8 10.4 %collective-permute-start.6 = (bf16[2,16,3200]{2,1,0:T(8,128)(2,1)S(1)}, bf16[2,16,3200]{2,1,0:T(8,128)(2,1)S(1)}, u32[]{:S(2)}, u32[]{:S(2)}) collective-permute-start(bf16[2,16,3200]{2,1,0:T(8,128)(2,1)S(1)} %pad_maximum_fusion), channel_id=1, source_target_pairs={{0,64},{32,96},{64,0},{96,32},{1,65},{33,97},{65,1},{97,33},{2,66}... | collective-permute-start | bytes 614408 | tf_op jit(solution)/shard_map/ppermute | solution.py:355
  13.5 10.7 %collective-permute-start.1 = (bf16[2,16,3200]{2,1,0:T(8,128)(2,1)S(1)}, bf16[2,16,3200]{2,1,0:T(8,128)(2,1)S(1)}, u32[]{:S(2)}, u32[]{:S(2)}) collective-permute-start(bf16[2,16,3200]{2,1,0:T(8,128)(2,1)S(1)} %pad_maximum_fusion), channel_id=1, source_target_pairs={{0,1},{1,0},{2,3},{3,2},{4,5},{5,4},{6,7},{7,6},{8,9},{9,8},{10,11... | collective-permute-start | bytes 614408 | tf_op jit(solution)/shard_map/ppermute | solution.py:32
  15.5 8.6 %collective-permute-start.3 = (bf16[2,16,3200]{2,1,0:T(8,128)(2,1)S(1)}, bf16[2,16,3200]{2,1,0:T(8,128)(2,1)S(1)}, u32[]{:S(2)}, u32[]{:S(2)}) collective-permute-start(bf16[2,16,3200]{2,1,0:T(8,128)(2,1)S(1)} %collective-permute-done.2), channel_id=1, source_target_pairs={{0,1},{1,0},{2,3},{3,2},{4,5},{5,4},{6,7},{7,6},{8,9},{9,8},{10,11... | collective-permute-start | bytes 614408 | tf_op jit(solution)/shard_map/ppermute | solution.py:32
  29.6 10.6 %collective-permute-start.8 = (bf16[2,96,1536]{2,1,0:T(8,128)(2,1)}, bf16[2,96,1536]{2,1,0:T(8,128)(2,1)S(1)}, u32[]{:S(2)}, u32[]{:S(2)}) collective-permute-start(bf16[2,96,1536]{2,1,0:T(8,128)(2,1)} %get-tuple-element.49.rest_0_), channel_id=1, source_target_pairs={{0,4},{1,13},{4,8},{5,1},{8,12},{9,5},{12,0},{13,9},{2,6},{3,15},{... | collective-permute-start | bytes 1769480 | tf_op jit(solution)/shard_map/ppermute | solution.py:23
  32.2 15.2 %collective-permute-start.10 = (bf16[2,96,1536]{2,1,0:T(8,128)(2,1)}, bf16[2,96,1536]{2,1,0:T(8,128)(2,1)S(1)}, u32[]{:S(2)}, u32[]{:S(2)}) collective-permute-start(bf16[2,96,1536]{2,1,0:T(8,128)(2,1)} %get-tuple-element.49.rest_0_), channel_id=1, source_target_pairs={{0,2},{2,0},{1,3},{3,1},{4,6},{6,4},{5,7},{7,5},{8,10},{10,8},{9,1... | collective-permute-start | bytes 1769480 | tf_op jit(solution)/shard_map/ppermute | solution.py:32
  32.2 15.2 %collective-permute-start.11 = (bf16[2,96,1536]{2,1,0:T(8,128)(2,1)}, bf16[2,96,1536]{2,1,0:T(8,128)(2,1)S(1)}, u32[]{:S(2)}, u32[]{:S(2)}) collective-permute-start(bf16[2,96,1536]{2,1,0:T(8,128)(2,1)} %get-tuple-element.50.rest_1_), channel_id=1, source_target_pairs={{0,4},{1,13},{4,8},{5,1},{8,12},{9,5},{12,0},{13,9},{2,6},{3,15},{... | collective-permute-start | bytes 1769480 | tf_op jit(solution)/shard_map/ppermute | solution.py:23
  48.4 12.8 %collective-permute-start.9 = (bf16[2,96,1536]{2,1,0:T(8,128)(2,1)S(1)}, bf16[2,96,1536]{2,1,0:T(8,128)(2,1)S(1)}, u32[]{:S(2)}, u32[]{:S(2)}) collective-permute-start(bf16[2,96,1536]{2,1,0:T(8,128)(2,1)S(1)} %collective-permute-done.8.rest_2_), channel_id=1, source_target_pairs={{0,4},{1,13},{4,8},{5,1},{8,12},{9,5},{12,0},{13,9},{2,6},{3,15},{... | collective-permute-start | bytes 1769480 | tf_op jit(solution)/shard_map/ppermute | solution.py:23
  49.5 14.9 %collective-permute-start.16 = (bf16[2,96,1536]{2,1,0:T(8,128)(2,1)S(1)}, bf16[2,96,1536]{2,1,0:T(8,128)(2,1)S(1)}, u32[]{:S(2)}, u32[]{:S(2)}) collective-permute-start(bf16[2,96,1536]{2,1,0:T(8,128)(2,1)S(1)} %collective-permute-done.8.rest_2_), channel_id=1, source_target_pairs={{0,2},{2,0},{1,3},{3,1},{4,6},{6,4},{5,7},{7,5},{8,10},{10,8},{9,1... | collective-permute-start | bytes 1769480 | tf_op jit(solution)/shard_map/ppermute | solution.py:32
  49.5 15.3 %collective-permute-start.18 = (bf16[2,96,1536]{2,1,0:T(8,128)(2,1)S(1)}, bf16[2,96,1536]{2,1,0:T(8,128)(2,1)S(1)}, u32[]{:S(2)}, u32[]{:S(2)}) collective-permute-start(bf16[2,96,1536]{2,1,0:T(8,128)(2,1)S(1)} %collective-permute-done.12.rest_1_), channel_id=1, source_target_pairs={{0,4},{1,13},{4,8},{5,1},{8,12},{9,5},{12,0},{13,9},{2,6},{3,15},{... | collective-permute-start | bytes 1769480 | tf_op jit(solution)/shard_map/ppermute | solution.py:23
  66.0 12.0 %collective-permute-start.17 = (bf16[2,64,1536]{2,1,0:T(8,128)(2,1)S(1)}, bf16[2,64,1536]{2,1,0:T(8,128)(2,1)S(1)}, u32[]{:S(2)}, u32[]{:S(2)}) collective-permute-start(bf16[2,64,1536]{2,1,0:T(8,128)(2,1)S(1)} %slice.13), channel_id=1, source_target_pairs={{0,4},{1,13},{4,8},{5,1},{8,12},{9,5},{12,0},{13,9},{2,6},{3,15},{... | collective-permute-start | bytes 1179656 | tf_op jit(solution)/shard_map/ppermute | solution.py:23
  66.4 11.6 %collective-permute-start.15 = (bf16[2,32,1536]{2,1,0:T(8,128)(2,1)S(1)}, bf16[2,32,1536]{2,1,0:T(8,128)(2,1)S(1)}, u32[]{:S(2)}, u32[]{:S(2)}) collective-permute-start(bf16[2,32,1536]{2,1,0:T(8,128)(2,1)S(1)} %slice.12), channel_id=1, source_target_pairs={{0,2},{2,0},{1,3},{3,1},{4,6},{6,4},{5,7},{7,5},{8,10},{10,8},{9,1... | collective-permute-start | bytes 589832 | tf_op jit(solution)/shard_map/ppermute | solution.py:32
  87.7 19.9 %collective-permute-start.27 = (bf16[2,1536,256]{2,1,0:T(8,128)(2,1)}, bf16[2,1536,256]{2,1,0:T(8,128)(2,1)}, u32[]{:S(2)}, u32[]{:S(2)}) collective-permute-start(bf16[2,1536,256]{2,1,0:T(8,128)(2,1)} %get-tuple-element.71.rest_0_.rest_1_), channel_id=1, source_target_pairs={{0,4},{1,13},{4,8},{5,1},{8,12},{9,5},{12,0},{13,9},{2,6},{3,15},{... | collective-permute-start | bytes 4718600 | tf_op jit(solution)/shard_map/ppermute | solution.py:23
  89.3 36.8 %collective-permute-start.25 = (bf16[2,1536,256]{2,1,0:T(8,128)(2,1)}, bf16[2,1536,256]{2,1,0:T(8,128)(2,1)S(1)}, u32[]{:S(2)}, u32[]{:S(2)}) collective-permute-start(bf16[2,1536,256]{2,1,0:T(8,128)(2,1)} %get-tuple-element.71.rest_0_.rest_1_), channel_id=1, source_target_pairs={{0,2},{2,0},{1,3},{3,1},{4,6},{6,4},{5,7},{7,5},{8,10},{10,8},{9,1... | collective-permute-start | bytes 4718600 | tf_op jit(solution)/shard_map/ppermute | solution.py:32
  91.2 34.9 %collective-permute-start.26 = (bf16[2,1536,256]{2,1,0:T(8,128)(2,1)S(1)}, bf16[2,1536,256]{2,1,0:T(8,128)(2,1)}, u32[]{:S(2)}, u32[]{:S(2)}) collective-permute-start(bf16[2,1536,256]{2,1,0:T(8,128)(2,1)S(1)} %collective-permute-done.24.rest_2_), channel_id=1, source_target_pairs={{0,4},{1,13},{4,8},{5,1},{8,12},{9,5},{12,0},{13,9},{2,6},{3,15},{... | collective-permute-start | bytes 4718600 | tf_op jit(solution)/shard_map/ppermute | solution.py:23
  126.9 7.9 %collective-permute-start.29 = (bf16[2,1536,256]{2,1,0:T(8,128)(2,1)}, bf16[2,1536,256]{2,1,0:T(8,128)(2,1)}, u32[]{:S(2)}, u32[]{:S(2)}) collective-permute-start(bf16[2,1536,256]{2,1,0:T(8,128)(2,1)} %collective-permute-done.26.rest_6_), channel_id=1, source_target_pairs={{0,1},{1,0},{2,3},{3,2},{4,5},{5,4},{6,7},{7,6},{8,9},{9,8},{10,11... | collective-permute-start | bytes 4718600 | tf_op jit(solution)/shard_map/ppermute | solution.py:32
  127.4 20.4 %collective-permute-start.31 = (bf16[2,1536,256]{2,1,0:T(8,128)(2,1)}, bf16[2,1536,256]{2,1,0:T(8,128)(2,1)S(1)}, u32[]{:S(2)}, u32[]{:S(2)}) collective-permute-start(bf16[2,1536,256]{2,1,0:T(8,128)(2,1)} %collective-permute-done.27.rest_5_), channel_id=1, source_target_pairs={{0,4},{1,13},{4,8},{5,1},{8,12},{9,5},{12,0},{13,9},{2,6},{3,15},{... | collective-permute-start | bytes 4718600 | tf_op jit(solution)/shard_map/ppermute | solution.py:23
  127.5 36.7 %collective-permute-start.33 = (bf16[2,1536,256]{2,1,0:T(8,128)(2,1)}, bf16[2,1536,256]{2,1,0:T(8,128)(2,1)S(1)}, u32[]{:S(2)}, u32[]{:S(2)}) collective-permute-start(bf16[2,1536,256]{2,1,0:T(8,128)(2,1)} %collective-permute-done.27.rest_5_), channel_id=1, source_target_pairs={{0,2},{2,0},{1,3},{3,1},{4,6},{6,4},{5,7},{7,5},{8,10},{10,8},{9,1... | collective-permute-start | bytes 4718600 | tf_op jit(solution)/shard_map/ppermute | solution.py:32
  132.2 32.6 %collective-permute-start.35 = (bf16[2,1536,256]{2,1,0:T(8,128)(2,1)}, bf16[2,1536,256]{2,1,0:T(8,128)(2,1)}, u32[]{:S(2)}, u32[]{:S(2)}) collective-permute-start(bf16[2,1536,256]{2,1,0:T(8,128)(2,1)} %collective-permute-done.28.rest_4_), channel_id=1, source_target_pairs={{0,4},{1,13},{4,8},{5,1},{8,12},{9,5},{12,0},{13,9},{2,6},{3,15},{... | collective-permute-start | bytes 4718600 | tf_op jit(solution)/shard_map/ppermute | solution.py:23
  164.8 7.5 %collective-permute-start.38 = (bf16[2,1536,256]{2,1,0:T(8,128)(2,1)S(1)}, bf16[2,1536,256]{2,1,0:T(8,128)(2,1)S(1)}, u32[]{:S(2)}, u32[]{:S(2)}) collective-permute-start(bf16[2,1536,256]{2,1,0:T(8,128)(2,1)S(1)} %collective-permute-done.31.rest_5_), channel_id=1, source_target_pairs={{0,1},{1,0},{2,3},{3,2},{4,5},{5,4},{6,7},{7,6},{8,9},{9,8},{10,11... | collective-permute-start | bytes 4718600 | tf_op jit(solution)/shard_map/ppermute | solution.py:32
  164.8 7.7 %collective-permute-start.36 = (bf16[2,1536,256]{2,1,0:T(8,128)(2,1)}, bf16[2,1536,256]{2,1,0:T(8,128)(2,1)S(1)}, u32[]{:S(2)}, u32[]{:S(2)}) collective-permute-start(bf16[2,1536,256]{2,1,0:T(8,128)(2,1)} %collective-permute-done.35.rest_2_), channel_id=1, source_target_pairs={{0,1},{1,0},{2,3},{3,2},{4,5},{5,4},{6,7},{7,6},{8,9},{9,8},{10,11... | collective-permute-start | bytes 4718600 | tf_op jit(solution)/shard_map/ppermute | solution.py:32
  167.2 17.0 %collective-permute-start.34 = (bf16[2,1024,256]{2,1,0:T(8,128)(2,1)}, bf16[2,1024,256]{2,1,0:T(8,128)(2,1)}, u32[]{:S(2)}, u32[]{:S(2)}) collective-permute-start(bf16[2,1024,256]{2,1,0:T(8,128)(2,1)} %slice.15), channel_id=1, source_target_pairs={{0,4},{1,13},{4,8},{5,1},{8,12},{9,5},{12,0},{13,9},{2,6},{3,15},{... | collective-permute-start | bytes 3145736 | tf_op jit(solution)/shard_map/ppermute | solution.py:23
  168.1 16.1 %collective-permute-start.32 = (bf16[2,512,256]{2,1,0:T(8,128)(2,1)}, bf16[2,512,256]{2,1,0:T(8,128)(2,1)}, u32[]{:S(2)}, u32[]{:S(2)}) collective-permute-start(bf16[2,512,256]{2,1,0:T(8,128)(2,1)} %slice.14), channel_id=1, source_target_pairs={{0,2},{2,0},{1,3},{3,1},{4,6},{6,4},{5,7},{7,5},{8,10},{10,8},{9,1... | collective-permute-start | bytes 1572872 | tf_op jit(solution)/shard_map/ppermute | solution.py:32
  (52 other events, 275.9 us)

commit v3 on v2

--- a/solution.py
+++ b/solution.py
@@ -287,8 +287,8 @@
 
 
 class Spread:
-    def __init__(self):
-        self.found = {}
+    def __init__(self, share):
+        self.found, self.share = {}, share
 
     def keep(self, arrays, at, dl, core):
         twins = [swap(array, "c") for array in arrays]
@@ -320,15 +320,15 @@
     def third(self, token):
         far, near_beside, beside_near = self.moved
         far, token = tie(far, token)
-        rows = far.shape[1] // 3
-        over_l = swap(far[:, :rows], "l")
+        rows = far.shape[1] // self.share if self.share else 0
+        over_l = (swap(far[:, :rows], "l"),) if rows else ()
         near_beside, token = tie(near_beside, token)
-        over_x = ring_hop(near_beside[:, rows:], "x")
+        over_x = ring_hop(near_beside[:, rows:] if rows else near_beside, "x")
         self.keep([near_beside], "m", 1, 0)
         beside_near, token = tie(beside_near, token)
         self.keep([beside_near], "m", 1, 1)
         self.keep([far], "f", 0, 0)
-        self.moved = (over_l, over_x)
+        self.moved = over_l + (over_x,)
         return token
 
     def end(self, token):
@@ -389,7 +389,7 @@
         return ffn(offsets, place_in(chips), found, gate_panel, up_panel, total, token, old)
 
     token = jnp.zeros((8, 128), jnp.float32)
-    rows = Spread()
+    rows = Spread(0)
     rows.open(pair, twin)
     hidden, token = hidden_of([("o", 0)], token)
     token = rows.first(token)
@@ -403,7 +403,7 @@
         found = blocks_of(panels, chips)
         return gram(ids, place_in(chips), scale, own, found, features, token, old)
 
-    panels = Spread()
+    panels = Spread(3)
     panels.open(hidden)
     token = panels.first(token)
     own = hidden

time: 196 us -> 195 us (level)
  starting transfers between devices: 38.1 us -> 33.9 us
  waiting for transfers between devices: 80.2 us -> 84.1 us
    ppermute x27 -> x25, waiting for transfers between devices: 60.4 us -> 64.1 us  [swap(): return lax.ppermute(a, axis, [(0, 1), (1, 0)])]
    ppermute x27 -> x25, starting transfers between devices: 20.3 us -> 16.8 us  [swap(): return lax.ppermute(a, axis, [(0, 1), (1, 0)])]
    unnamed x71 -> x67, local copies, waits for them, and re-layouts: 5.29 us -> 5.34 us
  transfers between devices with their start and end apart: 41 -> 39, of which waited for: 19 -> 20; matrix products, arithmetic and copies ran while one was open for 2% -> 2% of each run, Pallas kernels for 24% -> 24%
where the time goes in v3:
time: 195 us
  waiting for transfers between devices  84.1 us (43%)
  Pallas kernels  64.3 us (33%)
  starting transfers between devices  33.9 us (17%)
  local copies, waits for them, and re-layouts  8.75 us (4%)
  other arithmetic  2.83 us (1%)
    ppermute x25, waiting for transfers between devices, swap(): return lax.ppermute(a, axis, [(0, 1), (1, 0)])  64.1 us
    pallas_call x4, Pallas kernels, ffn(): pl.pallas_call(functools.partial(ffn_kernel, sources, first, len(arrays),...  30.9 us
    pallas_call x3, Pallas kernels, gram(): pl.pallas_call(functools.partial(gram_kernel, sources, start, len(arrays)...  29.4 us
    ppermute x25, starting transfers between devices, swap(): return lax.ppermute(a, axis, [(0, 1), (1, 0)])  16.8 us
    ppermute x11, waiting for transfers between devices, ring_hop(): return lax.ppermute(a, (axis, 'c'), pairs)  15.4 us
    ppermute x11, starting transfers between devices, ring_hop(): return lax.ppermute(a, (axis, 'c'), pairs)  10.8 us
    unnamed x67, local copies, waits for them, and re-layouts  5.34 us
    ppermute x1, starting transfers between devices, far_swap(): return lax.ppermute(a, ('h', 'l'), [(0, 3), (3, 0), (1, 2), (2, 1)])  4.67 us
  transfers between devices with their start and end apart: 39, of which 20 were waited for; matrix products, arithmetic and copies ran while one was open for 2% of the time, Pallas kernels for 24%

profile of v3, /device:TPU:1, one launch (start us, length us, event | category | flops | bytes accessed | tf_op | source)
XLA Modules:
  0.0 195.2 jit_solution(3315141709003537348)
XLA Ops:
  1.7 4.7 %collective-permute-start = (bf16[16,3200]{1,0:T(8,128)(2,1)S(1)}, bf16[16,3200]{1,0:T(8,128)(2,1)S(1)}, u32[]{:S(2)}, u32[]{:S(2)}) collective-permute-start(bf16[16,3200]{1,0:T(8,128)(2,1)S(1)} %get-tuple-element.92), channel_id=1, source_target_pairs={{0,18},{18,0},{2,16},{16,2},{1,19},{19,1},{3,17},{17,3},{4,22},{22... | collective-permute-start | bytes 307208 | tf_op jit(solution)/shard_map/ppermute | solution.py:36
  6.4 2.6 %collective-permute-done = bf16[16,3200]{1,0:T(8,128)(2,1)S(1)} collective-permute-done((bf16[16,3200]{1,0:T(8,128)(2,1)S(1)}, bf16[16,3200]{1,0:T(8,128)(2,1)S(1)}, u32[]{:S(2)}, u32[]{:S(2)}) %collective-permute-start) | collective-permute-done | bytes 102432 | tf_op jit(solution)/shard_map/ppermute | solution.py:36
  9.0 2.8 %collective-permute-start.2 = (bf16[2,16,3200]{2,1,0:T(8,128)(2,1)S(1)}, bf16[2,16,3200]{2,1,0:T(8,128)(2,1)S(1)}, u32[]{:S(2)}, u32[]{:S(2)}) collective-permute-start(bf16[2,16,3200]{2,1,0:T(8,128)(2,1)S(1)} %pad_maximum_fusion), channel_id=1, source_target_pairs={{0,32},{1,97},{32,64},{33,1},{64,96},{65,33},{96,0},{97,65},{2,34}... | collective-permute-start | bytes 614408 | tf_op jit(solution)/shard_map/ppermute | solution.py:23
  13.5 2.1 %collective-permute-start.1 = (bf16[2,16,3200]{2,1,0:T(8,128)(2,1)S(1)}, bf16[2,16,3200]{2,1,0:T(8,128)(2,1)S(1)}, u32[]{:S(2)}, u32[]{:S(2)}) collective-permute-start(bf16[2,16,3200]{2,1,0:T(8,128)(2,1)S(1)} %pad_maximum_fusion), channel_id=1, source_target_pairs={{0,1},{1,0},{2,3},{3,2},{4,5},{5,4},{6,7},{7,6},{8,9},{9,8},{10,11... | collective-permute-start | bytes 614408 | tf_op jit(solution)/shard_map/ppermute | solution.py:32
  15.5 3.1 %collective-permute-start.3 = (bf16[2,16,3200]{2,1,0:T(8,128)(2,1)S(1)}, bf16[2,16,3200]{2,1,0:T(8,128)(2,1)S(1)}, u32[]{:S(2)}, u32[]{:S(2)}) collective-permute-start(bf16[2,16,3200]{2,1,0:T(8,128)(2,1)S(1)} %collective-permute-done.2), channel_id=1, source_target_pairs={{0,1},{1,0},{2,3},{3,2},{4,5},{5,4},{6,7},{7,6},{8,9},{9,8},{10,11... | collective-permute-start | bytes 614408 | tf_op jit(solution)/shard_map/ppermute | solution.py:32
  25.6 4.0 %shard_map.55 = (bf16[2,96,1536]{2,1,0:T(8,128)(2,1)}, bf16[2,96,1536]{2,1,0:T(8,128)(2,1)}) custom-call(s32[1]{0:T(128)} %bitcast.17.expert_ref, f32[8,256]{1,0:T(8,128)} %broadcast_in_dim.18.base_ref, bf16[32,3200]{1,0:T(8,128)(2,1)} %bitcast.48, bf16[32,3200]{1,0:T(8,128)(2,1)} %bitcast.53, bf16[32,3200]{1,0:T(8,128)(2,1)} %bitcast.50, ...), custom_call_target="tpu_custom_call" | custom-call | flops 3449999872 | bytes 1000000 | tf_op jit(solution)/shard_map/pallas_call | solution.py:90
  29.6 2.5 %collective-permute-start.8 = (bf16[2,96,1536]{2,1,0:T(8,128)(2,1)}, bf16[2,96,1536]{2,1,0:T(8,128)(2,1)S(1)}, u32[]{:S(2)}, u32[]{:S(2)}) collective-permute-start(bf16[2,96,1536]{2,1,0:T(8,128)(2,1)} %get-tuple-element.48.rest_0_), channel_id=1, source_target_pairs={{0,4},{1,13},{4,8},{5,1},{8,12},{9,5},{12,0},{13,9},{2,6},{3,15},{... | collective-permute-start | bytes 1769480 | tf_op jit(solution)/shard_map/ppermute | solution.py:23
  34.0 6.2 %shard_map.56 = (bf16[2,1536,256]{2,1,0:T(8,128)(2,1)}, f32[8,128]{1,0:T(8,128)}) custom-call(s32[16]{0:T(128)} %broadcast_multiply_fusion.offsets_ref, bf16[2,96,1536]{2,1,0:T(8,128)(2,1)} %get-tuple-element.48.rest_0_, bf16[2,96,1536]{2,1,0:T(8,128)(2,1)} %get-tuple-element.49.rest_1_, bf16[3072,512]{1,0:T(8,128)(2,1)} %bitcast.40, ...), custom_call_target="tpu_custom_call" | custom-call | flops 1150000000 | bytes 1000000 | tf_op jit(solution)/shard_map/pallas_call | solution.py:191
  40.3 7.1 %collective-permute-done.11.rest_0_ = bf16[2,96,1536]{2,1,0:T(8,128)(2,1)S(1)} collective-permute-done((bf16[2,96,1536]{2,1,0:T(8,128)(2,1)}, bf16[2,96,1536]{2,1,0:T(8,128)(2,1)S(1)}, u32[]{:S(2)}, u32[]{:S(2)}) %collective-permute-start.11) | collective-permute-done | bytes 589856 | tf_op jit(solution)/shard_map/ppermute | solution.py:32
  52.0 9.1 %shard_map.57 = (bf16[2,1536,256]{2,1,0:T(8,128)(2,1)}, f32[8,128]{1,0:T(8,128)}) custom-call(s32[16]{0:T(128)} %broadcast_multiply_fusion.offsets_ref, bf16[2,96,1536]{2,1,0:T(8,128)(2,1)} %copy-done.11, bf16[2,96,1536]{2,1,0:T(8,128)(2,1)} %copy-done.16, bf16[2,96,1536]{2,1,0:T(8,128)(2,1)} %copy-done.10, ...), custom_call_target="tpu_custom_call", output_to_operand_aliasing={{0}: (10, {})} | custom-call | flops 1150000000 | bytes 1000000 | tf_op jit(solution)/shard_map/pallas_call | solution.py:191
  61.2 3.1 %collective-permute-done.9.rest_0_ = bf16[2,96,1536]{2,1,0:T(8,128)(2,1)S(1)} collective-permute-done((bf16[2,96,1536]{2,1,0:T(8,128)(2,1)S(1)}, bf16[2,96,1536]{2,1,0:T(8,128)(2,1)S(1)}, u32[]{:S(2)}, u32[]{:S(2)}) %collective-permute-start.9) | collective-permute-done | bytes 589856 | tf_op jit(solution)/shard_map/ppermute | solution.py:32
  68.9 9.1 %shard_map.58 = (bf16[2,1536,256]{2,1,0:T(8,128)(2,1)}, f32[8,128]{1,0:T(8,128)}) custom-call(s32[16]{0:T(128)} %broadcast_multiply_fusion.offsets_ref, bf16[2,96,1536]{2,1,0:T(8,128)(2,1)} %copy-done.13, bf16[2,96,1536]{2,1,0:T(8,128)(2,1)} %copy-done.15, bf16[2,96,1536]{2,1,0:T(8,128)(2,1)} %copy-done.21, ...), custom_call_target="tpu_custom_call", output_to_operand_aliasing={{0}: (10, {})} | custom-call | flops 1150000000 | bytes 1000000 | tf_op jit(solution)/shard_map/pallas_call | solution.py:191
  81.0 6.4 %shard_map.59 = (bf16[2,1536,256]{2,1,0:T(8,128)(2,1)}, f32[8,128]{1,0:T(8,128)}) custom-call(s32[16]{0:T(128)} %broadcast_multiply_fusion.offsets_ref, bf16[2,96,1536]{2,1,0:T(8,128)(2,1)} %copy-done.8, bf16[2,96,1536]{2,1,0:T(8,128)(2,1)} %copy-done.9, bf16[3072,512]{1,0:T(8,128)(2,1)} %bitcast.43, ...), custom_call_target="tpu_custom_call", output_to_operand_aliasing={{0}: (6, {})} | custom-call | flops 1150000000 | bytes 1000000 | tf_op jit(solution)/shard_map/pallas_call | solution.py:191
  88.9 2.2 %collective-permute-done.22.rest_2_ = bf16[2,1536,256]{2,1,0:T(8,128)(2,1)S(1)} collective-permute-done((bf16[2,1536,256]{2,1,0:T(8,128)(2,1)}, bf16[2,1536,256]{2,1,0:T(8,128)(2,1)S(1)}, u32[]{:S(2)}, u32[]{:S(2)}) %collective-permute-start.22) | collective-permute-done | bytes 1572896 | tf_op jit(solution)/shard_map/ppermute | solution.py:32
  92.1 15.3 %collective-permute-done.25.rest_5_ = bf16[2,1536,256]{2,1,0:T(8,128)(2,1)} collective-permute-done((bf16[2,1536,256]{2,1,0:T(8,128)(2,1)}, bf16[2,1536,256]{2,1,0:T(8,128)(2,1)}, u32[]{:S(2)}, u32[]{:S(2)}) %collective-permute-start.25) | collective-permute-done | bytes 1572896 | tf_op jit(solution)/shard_map/ppermute | solution.py:23
  107.5 17.4 %collective-permute-done.23.rest_3_ = bf16[2,1536,256]{2,1,0:T(8,128)(2,1)S(1)} collective-permute-done((bf16[2,1536,256]{2,1,0:T(8,128)(2,1)}, bf16[2,1536,256]{2,1,0:T(8,128)(2,1)S(1)}, u32[]{:S(2)}, u32[]{:S(2)}) %collective-permute-start.23) | collective-permute-done | bytes 1572896 | tf_op jit(solution)/shard_map/ppermute | solution.py:32
  124.9 1.9 collective-permute-start.26
  127.4 4.8 %collective-permute-done.26.rest_4_ = bf16[2,1536,256]{2,1,0:T(8,128)(2,1)} collective-permute-done((bf16[2,1536,256]{2,1,0:T(8,128)(2,1)S(1)}, bf16[2,1536,256]{2,1,0:T(8,128)(2,1)}, u32[]{:S(2)}, u32[]{:S(2)}) %collective-permute-start.26) | collective-permute-done | bytes 1572896 | tf_op jit(solution)/shard_map/ppermute | solution.py:32
  134.6 13.0 %shard_map.60 = (f32[512,8192]{1,0:T(8,128)}, f32[8,128]{1,0:T(8,128)}, bf16[512,1536]{1,0:T(8,128)(2,1)}) custom-call(s32[16]{0:T(128)} %copy-done.24, f32[1]{0:T(128)} %bitcast.16.scale_ref, bf16[2,1536,256]{2,1,0:T(8,128)(2,1)} %get-tuple-element.69.rest_0_.rest_1_, bf16[2,1536,256]{2,1,0:T(8,128)(2,1)} %get-tuple-element.69.rest_0_.rest_1_, ...), custom_call_target="tpu_custom_call" | custom-call | flops 1150000000 | bytes 1000000 | tf_op jit(solution)/shard_map/pallas_call | solution.py:265
  147.6 16.0 %collective-permute-done.31.rest_1_ = bf16[2,1536,256]{2,1,0:T(8,128)(2,1)S(1)} collective-permute-done((bf16[2,1536,256]{2,1,0:T(8,128)(2,1)}, bf16[2,1536,256]{2,1,0:T(8,128)(2,1)S(1)}, u32[]{:S(2)}, u32[]{:S(2)}) %collective-permute-start.31) | collective-permute-done | bytes 1572896 | tf_op jit(solution)/shard_map/ppermute | solution.py:32
  168.0 3.9 %collective-permute-done.36.rest_6_ = bf16[2,1536,256]{2,1,0:T(8,128)(2,1)S(1)} collective-permute-done((bf16[2,1536,256]{2,1,0:T(8,128)(2,1)S(1)}, bf16[2,1536,256]{2,1,0:T(8,128)(2,1)S(1)}, u32[]{:S(2)}, u32[]{:S(2)}) %collective-permute-start.36) | collective-permute-done | bytes 1572896 | tf_op jit(solution)/shard_map/ppermute | solution.py:32
  173.6 10.1 %shard_map.61 = (f32[512,8192]{1,0:T(8,128)}, f32[8,128]{1,0:T(8,128)}) custom-call(s32[16]{0:T(128)} %copy-done.24, f32[1]{0:T(128)} %bitcast.16.scale_ref, bf16[512,1536]{1,0:T(8,128)(2,1)} %get-tuple-element.76.rest_0_, bf16[2,1536,256]{2,1,0:T(8,128)(2,1)} %copy-done, ...), custom_call_target="tpu_custom_call", output_to_operand_aliasing={{0}: (10, {})} | custom-call | flops 1150000000 | bytes 1000000 | tf_op jit(solution)/shard_map/pallas_call | solution.py:265
  184.4 3.1 %collective-permute-done.37.rest_3_ = bf16[2,512,256]{2,1,0:T(8,128)(2,1)S(1)} collective-permute-done((bf16[2,512,256]{2,1,0:T(8,128)(2,1)}, bf16[2,512,256]{2,1,0:T(8,128)(2,1)S(1)}, u32[]{:S(2)}, u32[]{:S(2)}) %collective-permute-start.37) | collective-permute-done | bytes 524320 | tf_op jit(solution)/shard_map/ppermute | solution.py:32
  188.7 6.3 %shard_map.62 = (f32[512,8192]{1,0:T(8,128)}, f32[8,128]{1,0:T(8,128)}) custom-call(s32[16]{0:T(128)} %copy-done.24, f32[1]{0:T(128)} %bitcast.16.scale_ref, bf16[512,1536]{1,0:T(8,128)(2,1)} %get-tuple-element.76.rest_0_, bf16[2,512,256]{2,1,0:T(8,128)(2,1)} %collective-permute-done.30.rest_1_, ...), custom_call_target="tpu_custom_call", output_to_operand_aliasing={{0}: (8, {})} | custom-call | flops 1150000000 | bytes 1000000 | tf_op jit(solution)/shard_map/pallas_call | solution.py:265
  (143 shorter events, 36.9 us)
Async XLA Ops:
  1.7 7.3 %collective-permute-start = (bf16[16,3200]{1,0:T(8,128)(2,1)S(1)}, bf16[16,3200]{1,0:T(8,128)(2,1)S(1)}, u32[]{:S(2)}, u32[]{:S(2)}) collective-permute-start(bf16[16,3200]{1,0:T(8,128)(2,1)S(1)} %get-tuple-element.92), channel_id=1, source_target_pairs={{0,18},{18,0},{2,16},{16,2},{1,19},{19,1},{3,17},{17,3},{4,22},{22... | collective-permute-start | bytes 307208 | tf_op jit(solution)/shard_map/ppermute | solution.py:36
  11.8 8.2 %collective-permute-start.4 = (bf16[2,16,3200]{2,1,0:T(8,128)(2,1)S(1)}, bf16[2,16,3200]{2,1,0:T(8,128)(2,1)S(1)}, u32[]{:S(2)}, u32[]{:S(2)}) collective-permute-start(bf16[2,16,3200]{2,1,0:T(8,128)(2,1)S(1)} %pad_maximum_fusion), channel_id=1, source_target_pairs={{0,96},{1,33},{32,0},{33,65},{64,32},{65,97},{96,64},{97,1},{2,98}... | collective-permute-start | bytes 614408 | tf_op jit(solution)/shard_map/ppermute | solution.py:28
  11.8 10.4 %collective-permute-start.6 = (bf16[2,16,3200]{2,1,0:T(8,128)(2,1)S(1)}, bf16[2,16,3200]{2,1,0:T(8,128)(2,1)S(1)}, u32[]{:S(2)}, u32[]{:S(2)}) collective-permute-start(bf16[2,16,3200]{2,1,0:T(8,128)(2,1)S(1)} %pad_maximum_fusion), channel_id=1, source_target_pairs={{0,64},{32,96},{64,0},{96,32},{1,65},{33,97},{65,1},{97,33},{2,66}... | collective-permute-start | bytes 614408 | tf_op jit(solution)/shard_map/ppermute | solution.py:355
  13.5 10.7 %collective-permute-start.1 = (bf16[2,16,3200]{2,1,0:T(8,128)(2,1)S(1)}, bf16[2,16,3200]{2,1,0:T(8,128)(2,1)S(1)}, u32[]{:S(2)}, u32[]{:S(2)}) collective-permute-start(bf16[2,16,3200]{2,1,0:T(8,128)(2,1)S(1)} %pad_maximum_fusion), channel_id=1, source_target_pairs={{0,1},{1,0},{2,3},{3,2},{4,5},{5,4},{6,7},{7,6},{8,9},{9,8},{10,11... | collective-permute-start | bytes 614408 | tf_op jit(solution)/shard_map/ppermute | solution.py:32
  15.5 8.6 %collective-permute-start.3 = (bf16[2,16,3200]{2,1,0:T(8,128)(2,1)S(1)}, bf16[2,16,3200]{2,1,0:T(8,128)(2,1)S(1)}, u32[]{:S(2)}, u32[]{:S(2)}) collective-permute-start(bf16[2,16,3200]{2,1,0:T(8,128)(2,1)S(1)} %collective-permute-done.2), channel_id=1, source_target_pairs={{0,1},{1,0},{2,3},{3,2},{4,5},{5,4},{6,7},{7,6},{8,9},{9,8},{10,11... | collective-permute-start | bytes 614408 | tf_op jit(solution)/shard_map/ppermute | solution.py:32
  29.6 10.6 %collective-permute-start.8 = (bf16[2,96,1536]{2,1,0:T(8,128)(2,1)}, bf16[2,96,1536]{2,1,0:T(8,128)(2,1)S(1)}, u32[]{:S(2)}, u32[]{:S(2)}) collective-permute-start(bf16[2,96,1536]{2,1,0:T(8,128)(2,1)} %get-tuple-element.48.rest_0_), channel_id=1, source_target_pairs={{0,4},{1,13},{4,8},{5,1},{8,12},{9,5},{12,0},{13,9},{2,6},{3,15},{... | collective-permute-start | bytes 1769480 | tf_op jit(solution)/shard_map/ppermute | solution.py:23
  32.2 15.2 %collective-permute-start.11 = (bf16[2,96,1536]{2,1,0:T(8,128)(2,1)}, bf16[2,96,1536]{2,1,0:T(8,128)(2,1)S(1)}, u32[]{:S(2)}, u32[]{:S(2)}) collective-permute-start(bf16[2,96,1536]{2,1,0:T(8,128)(2,1)} %get-tuple-element.48.rest_0_), channel_id=1, source_target_pairs={{0,2},{2,0},{1,3},{3,1},{4,6},{6,4},{5,7},{7,5},{8,10},{10,8},{9,1... | collective-permute-start | bytes 1769480 | tf_op jit(solution)/shard_map/ppermute | solution.py:32
  32.2 15.2 %collective-permute-start.12 = (bf16[2,96,1536]{2,1,0:T(8,128)(2,1)}, bf16[2,96,1536]{2,1,0:T(8,128)(2,1)S(1)}, u32[]{:S(2)}, u32[]{:S(2)}) collective-permute-start(bf16[2,96,1536]{2,1,0:T(8,128)(2,1)} %get-tuple-element.49.rest_1_), channel_id=1, source_target_pairs={{0,4},{1,13},{4,8},{5,1},{8,12},{9,5},{12,0},{13,9},{2,6},{3,15},{... | collective-permute-start | bytes 1769480 | tf_op jit(solution)/shard_map/ppermute | solution.py:23
  48.4 12.8 %collective-permute-start.10 = (bf16[2,96,1536]{2,1,0:T(8,128)(2,1)S(1)}, bf16[2,96,1536]{2,1,0:T(8,128)(2,1)S(1)}, u32[]{:S(2)}, u32[]{:S(2)}) collective-permute-start(bf16[2,96,1536]{2,1,0:T(8,128)(2,1)S(1)} %collective-permute-done.8.rest_2_), channel_id=1, source_target_pairs={{0,4},{1,13},{4,8},{5,1},{8,12},{9,5},{12,0},{13,9},{2,6},{3,15},{... | collective-permute-start | bytes 1769480 | tf_op jit(solution)/shard_map/ppermute | solution.py:23
  49.5 14.9 %collective-permute-start.9 = (bf16[2,96,1536]{2,1,0:T(8,128)(2,1)S(1)}, bf16[2,96,1536]{2,1,0:T(8,128)(2,1)S(1)}, u32[]{:S(2)}, u32[]{:S(2)}) collective-permute-start(bf16[2,96,1536]{2,1,0:T(8,128)(2,1)S(1)} %collective-permute-done.8.rest_2_), channel_id=1, source_target_pairs={{0,2},{2,0},{1,3},{3,1},{4,6},{6,4},{5,7},{7,5},{8,10},{10,8},{9,1... | collective-permute-start | bytes 1769480 | tf_op jit(solution)/shard_map/ppermute | solution.py:32
  49.5 15.3 %collective-permute-start.17 = (bf16[2,96,1536]{2,1,0:T(8,128)(2,1)S(1)}, bf16[2,96,1536]{2,1,0:T(8,128)(2,1)S(1)}, u32[]{:S(2)}, u32[]{:S(2)}) collective-permute-start(bf16[2,96,1536]{2,1,0:T(8,128)(2,1)S(1)} %collective-permute-done.13.rest_1_), channel_id=1, source_target_pairs={{0,4},{1,13},{4,8},{5,1},{8,12},{9,5},{12,0},{13,9},{2,6},{3,15},{... | collective-permute-start | bytes 1769480 | tf_op jit(solution)/shard_map/ppermute | solution.py:23
  66.0 12.0 %collective-permute-start.16 = (bf16[2,96,1536]{2,1,0:T(8,128)(2,1)S(1)}, bf16[2,96,1536]{2,1,0:T(8,128)(2,1)S(1)}, u32[]{:S(2)}, u32[]{:S(2)}) collective-permute-start(bf16[2,96,1536]{2,1,0:T(8,128)(2,1)S(1)} %collective-permute-done.9.rest_0_), channel_id=1, source_target_pairs={{0,4},{1,13},{4,8},{5,1},{8,12},{9,5},{12,0},{13,9},{2,6},{3,15},{... | collective-permute-start | bytes 1769480 | tf_op jit(solution)/shard_map/ppermute | solution.py:23
  87.6 19.9 %collective-permute-start.25 = (bf16[2,1536,256]{2,1,0:T(8,128)(2,1)}, bf16[2,1536,256]{2,1,0:T(8,128)(2,1)}, u32[]{:S(2)}, u32[]{:S(2)}) collective-permute-start(bf16[2,1536,256]{2,1,0:T(8,128)(2,1)} %get-tuple-element.69.rest_0_.rest_1_), channel_id=1, source_target_pairs={{0,4},{1,13},{4,8},{5,1},{8,12},{9,5},{12,0},{13,9},{2,6},{3,15},{... | collective-permute-start | bytes 4718600 | tf_op jit(solution)/shard_map/ppermute | solution.py:23
  88.9 36.0 %collective-permute-start.23 = (bf16[2,1536,256]{2,1,0:T(8,128)(2,1)}, bf16[2,1536,256]{2,1,0:T(8,128)(2,1)S(1)}, u32[]{:S(2)}, u32[]{:S(2)}) collective-permute-start(bf16[2,1536,256]{2,1,0:T(8,128)(2,1)} %get-tuple-element.69.rest_0_.rest_1_), channel_id=1, source_target_pairs={{0,2},{2,0},{1,3},{3,1},{4,6},{6,4},{5,7},{7,5},{8,10},{10,8},{9,1... | collective-permute-start | bytes 4718600 | tf_op jit(solution)/shard_map/ppermute | solution.py:32
  91.1 33.8 %collective-permute-start.24 = (bf16[2,1536,256]{2,1,0:T(8,128)(2,1)S(1)}, bf16[2,1536,256]{2,1,0:T(8,128)(2,1)}, u32[]{:S(2)}, u32[]{:S(2)}) collective-permute-start(bf16[2,1536,256]{2,1,0:T(8,128)(2,1)S(1)} %collective-permute-done.22.rest_2_), channel_id=1, source_target_pairs={{0,4},{1,13},{4,8},{5,1},{8,12},{9,5},{12,0},{13,9},{2,6},{3,15},{... | collective-permute-start | bytes 4718600 | tf_op jit(solution)/shard_map/ppermute | solution.py:23
  124.9 7.3 %collective-permute-start.26 = (bf16[2,1536,256]{2,1,0:T(8,128)(2,1)S(1)}, bf16[2,1536,256]{2,1,0:T(8,128)(2,1)}, u32[]{:S(2)}, u32[]{:S(2)}) collective-permute-start(bf16[2,1536,256]{2,1,0:T(8,128)(2,1)S(1)} %collective-permute-done.23.rest_3_), channel_id=1, source_target_pairs={{0,1},{1,0},{2,3},{3,2},{4,5},{5,4},{6,7},{7,6},{8,9},{9,8},{10,11... | collective-permute-start | bytes 4718600 | tf_op jit(solution)/shard_map/ppermute | solution.py:32
  126.8 7.9 %collective-permute-start.27 = (bf16[2,1536,256]{2,1,0:T(8,128)(2,1)}, bf16[2,1536,256]{2,1,0:T(8,128)(2,1)}, u32[]{:S(2)}, u32[]{:S(2)}) collective-permute-start(bf16[2,1536,256]{2,1,0:T(8,128)(2,1)} %collective-permute-done.24.rest_6_), channel_id=1, source_target_pairs={{0,1},{1,0},{2,3},{3,2},{4,5},{5,4},{6,7},{7,6},{8,9},{9,8},{10,11... | collective-permute-start | bytes 4718600 | tf_op jit(solution)/shard_map/ppermute | solution.py:32
  127.3 20.4 %collective-permute-start.29 = (bf16[2,1536,256]{2,1,0:T(8,128)(2,1)}, bf16[2,1536,256]{2,1,0:T(8,128)(2,1)S(1)}, u32[]{:S(2)}, u32[]{:S(2)}) collective-permute-start(bf16[2,1536,256]{2,1,0:T(8,128)(2,1)} %collective-permute-done.25.rest_5_), channel_id=1, source_target_pairs={{0,4},{1,13},{4,8},{5,1},{8,12},{9,5},{12,0},{13,9},{2,6},{3,15},{... | collective-permute-start | bytes 4718600 | tf_op jit(solution)/shard_map/ppermute | solution.py:23
  127.3 36.4 %collective-permute-start.31 = (bf16[2,1536,256]{2,1,0:T(8,128)(2,1)}, bf16[2,1536,256]{2,1,0:T(8,128)(2,1)S(1)}, u32[]{:S(2)}, u32[]{:S(2)}) collective-permute-start(bf16[2,1536,256]{2,1,0:T(8,128)(2,1)} %collective-permute-done.25.rest_5_), channel_id=1, source_target_pairs={{0,2},{2,0},{1,3},{3,1},{4,6},{6,4},{5,7},{7,5},{8,10},{10,8},{9,1... | collective-permute-start | bytes 4718600 | tf_op jit(solution)/shard_map/ppermute | solution.py:32
  132.1 32.3 %collective-permute-start.33 = (bf16[2,1536,256]{2,1,0:T(8,128)(2,1)}, bf16[2,1536,256]{2,1,0:T(8,128)(2,1)}, u32[]{:S(2)}, u32[]{:S(2)}) collective-permute-start(bf16[2,1536,256]{2,1,0:T(8,128)(2,1)} %collective-permute-done.26.rest_4_), channel_id=1, source_target_pairs={{0,4},{1,13},{4,8},{5,1},{8,12},{9,5},{12,0},{13,9},{2,6},{3,15},{... | collective-permute-start | bytes 4718600 | tf_op jit(solution)/shard_map/ppermute | solution.py:23
  164.4 7.5 %collective-permute-start.36 = (bf16[2,1536,256]{2,1,0:T(8,128)(2,1)S(1)}, bf16[2,1536,256]{2,1,0:T(8,128)(2,1)S(1)}, u32[]{:S(2)}, u32[]{:S(2)}) collective-permute-start(bf16[2,1536,256]{2,1,0:T(8,128)(2,1)S(1)} %collective-permute-done.29.rest_5_), channel_id=1, source_target_pairs={{0,1},{1,0},{2,3},{3,2},{4,5},{5,4},{6,7},{7,6},{8,9},{9,8},{10,11... | collective-permute-start | bytes 4718600 | tf_op jit(solution)/shard_map/ppermute | solution.py:32
  164.4 7.7 %collective-permute-start.34 = (bf16[2,1536,256]{2,1,0:T(8,128)(2,1)}, bf16[2,1536,256]{2,1,0:T(8,128)(2,1)S(1)}, u32[]{:S(2)}, u32[]{:S(2)}) collective-permute-start(bf16[2,1536,256]{2,1,0:T(8,128)(2,1)} %collective-permute-done.33.rest_2_), channel_id=1, source_target_pairs={{0,1},{1,0},{2,3},{3,2},{4,5},{5,4},{6,7},{7,6},{8,9},{9,8},{10,11... | collective-permute-start | bytes 4718600 | tf_op jit(solution)/shard_map/ppermute | solution.py:32
  167.1 16.7 %collective-permute-start.32 = (bf16[2,1024,256]{2,1,0:T(8,128)(2,1)}, bf16[2,1024,256]{2,1,0:T(8,128)(2,1)}, u32[]{:S(2)}, u32[]{:S(2)}) collective-permute-start(bf16[2,1024,256]{2,1,0:T(8,128)(2,1)} %slice.7), channel_id=1, source_target_pairs={{0,4},{1,13},{4,8},{5,1},{8,12},{9,5},{12,0},{13,9},{2,6},{3,15},{... | collective-permute-start | bytes 3145736 | tf_op jit(solution)/shard_map/ppermute | solution.py:23
  167.9 15.8 %collective-permute-start.30 = (bf16[2,512,256]{2,1,0:T(8,128)(2,1)}, bf16[2,512,256]{2,1,0:T(8,128)(2,1)}, u32[]{:S(2)}, u32[]{:S(2)}) collective-permute-start(bf16[2,512,256]{2,1,0:T(8,128)(2,1)} %slice.6), channel_id=1, source_target_pairs={{0,2},{2,0},{1,3},{3,1},{4,6},{6,4},{5,7},{7,5},{8,10},{10,8},{9,1... | collective-permute-start | bytes 1572872 | tf_op jit(solution)/shard_map/ppermute | solution.py:32
  (48 other events, 266.3 us)
